TPU v7x, 32 devices: a whole 2x2x4 slice. The times are simulated.
32 devices in a mesh: dp: 16 (over z, y, x), fsdp: 2 (over core).
Axes of the slice: x: 2, y: 2, z: 4, core: 2. Of those that a mesh axis runs over, the one named last changes fastest.
Arguments:
- tokens: bfloat16 [128, 512, 768], P(('dp', 'fsdp')), may hold values from -6 to 6
- segment_ids: int32 [128, 512], P(('dp', 'fsdp')), may hold values from 0 to 3, never falling along the last dimension, each value on 1 to 256 neighbouring positions
- cotangent: bfloat16 [128, 512, 768], P(('dp', 'fsdp')), may hold values from -6 to 6
- w_proj: float32 [768, 1536], P(('dp', 'fsdp')), may hold values from -0.3125 to 0.3125
- w_point: float32 [768, 384], P(('dp', 'fsdp')), may hold values from -0.21875 to 0.21875
- w_out: float32 [768, 768], P(('dp', 'fsdp')), may hold values from -0.875 to 0.875
- w_up: float32 [2, 384, 1536], P(None, None, ('dp', 'fsdp')), may hold values from -0.3125 to 0.3125
- w_down: float32 [2, 1536, 384], P(None, ('dp', 'fsdp')), may hold values from -0.15625 to 0.15625
- proj_bias: float32 [4, 384], replicated, may hold values from -1.2 to 1.2
- conv_depth: float32 [9, 768], replicated, may hold values from -2 to 2
- kernel_weight: float32 [384, 54], replicated, may hold values from -0.3125 to 0.3125
- kernel_bias: float32 [54], replicated, may hold values from -3 to 3
- hidden_bias: float32 [4, 768], replicated, may hold values from -1.2 to 1.2
- up_bias: float32 [3072], replicated, may hold values from -1.2 to 1.2
- norm_gain: float32 [2, 768], replicated, may hold values from 0.25 to 1.75
Outputs:
- layer_out: bfloat16 [128, 512, 768], P(('dp', 'fsdp'))
- tokens_grad: float32 [128, 512, 768], P(('dp', 'fsdp'))
- w_proj_grad: float32 [768, 1536], P(('dp', 'fsdp'))
- w_point_grad: float32 [768, 384], P(('dp', 'fsdp'))
- w_out_grad: float32 [768, 768], P(('dp', 'fsdp'))
- w_up_grad: float32 [2, 384, 1536], P(None, None, ('dp', 'fsdp'))
- w_down_grad: float32 [2, 1536, 384], P(None, ('dp', 'fsdp'))
- proj_bias_grad: float32 [4, 384], replicated
- conv_depth_grad: float32 [9, 768], replicated
- kernel_weight_grad: float32 [384, 54], replicated
- kernel_bias_grad: float32 [54], replicated
- hidden_bias_grad: float32 [4, 768], replicated
- up_bias_grad: float32 [3072], replicated
- norm_gain_grad: float32 [2, 768], replicated
Inputs may be any that keep to these rules, and one draw needn't show every extreme that they name: `segment_ids`: document ids never fall along a row; each document holds 1 to 256 tokens, and one document of every row exactly 256.
All inputs are finite; a program needn't handle non-finite values.
Results may differ from a plain program's by a relative error of at most 0.012.
The roundings to bfloat16 on the way count: a program that leaves them out, or rounds other values in their place, can miss the bound.
Values may be sent and summed in bfloat16 or wider, within the bound.
No kernel may reach another device: no remote copies, remote signals or barrier semaphores. Data moves between devices by JAX's collectives and lax.ppermute only.
A program may use at most 256 MiB of HBM per device.

v0:
```python
import jax
import jax.numpy as jnp
from jax import lax
from jax.sharding import PartitionSpec as P

D = 768
FF = 3072
HEADS = 6
HEAD_DIM = 64
KERNEL = 9
GROUPS = 2
ATT = 384


precise = lax.Precision.HIGHEST
masked_score = -1000000000.0
norm_eps = 1e-12


def shifted(values, offset):
    half_width = KERNEL // 2
    widths = [(0, 0), (half_width, half_width)] + [(0, 0)] * (values.ndim - 2)
    padded = jnp.pad(values, widths)
    return lax.slice_in_dim(
        padded, half_width + offset, half_width + offset + values.shape[1], axis=1
    )


def tap_mask(segment_ids):
    half_width = KERNEL // 2
    padded = jnp.pad(segment_ids, ((0, 0), (half_width, half_width)), constant_values=-1)
    columns = [
        lax.slice_in_dim(padded, tap_index, tap_index + segment_ids.shape[1], axis=1) == segment_ids
        for tap_index in range(KERNEL)
    ]
    return jnp.stack(columns, axis=-1).astype(jnp.float32)


def norm_forward(values, gain_vec, bias_vec):
    row_mean = jnp.mean(values, axis=-1, keepdims=True)
    centered = values - row_mean
    variance = jnp.mean(centered * centered, axis=-1, keepdims=True)
    inv_std = lax.rsqrt(variance + norm_eps)
    normed = centered * inv_std
    return (normed * gain_vec + bias_vec, normed, inv_std)


def norm_backward(grad_out, normed, inv_std, gain_vec):
    grad_normed = grad_out * gain_vec
    grad_in = inv_std * (
        grad_normed
        - jnp.mean(grad_normed, axis=-1, keepdims=True)
        - normed * jnp.mean(grad_normed * normed, axis=-1, keepdims=True)
    )
    return (grad_in, jnp.sum(grad_out * normed, axis=(0, 1)), jnp.sum(grad_out, axis=(0, 1)))


def gelu_exact(values):
    return jax.nn.gelu(values, approximate=False)


def masked_scores(query_row, key_row, ids_row):
    scores = query_row.shape[-1] ** (-0.5) * jnp.einsum(
        "thd,uhd->htu", query_row, key_row, preferred_element_type=jnp.float32
    )
    same_doc = ids_row[:, None] == ids_row[None, :]
    return jnp.where(same_doc[None], scores, masked_score)


def attend_row(row_inputs):
    query_row, key_row, value_row, ids_row = row_inputs
    scores = masked_scores(query_row, key_row, ids_row)
    top_score = jnp.max(scores, axis=-1, keepdims=True)
    expo = jnp.exp(scores - top_score)
    total = jnp.sum(expo, axis=-1, keepdims=True)
    probs = expo / total
    context = jnp.einsum(
        "htu,uhd->thd", probs.astype(jnp.bfloat16), value_row, preferred_element_type=jnp.float32
    )
    return (context, (top_score + jnp.log(total))[..., 0])


def attend_back(row_inputs):
    query_row, key_row, value_row, ids_row, log_total, grad_context = row_inputs
    score_scale = query_row.shape[-1] ** (-0.5)
    probs = jnp.exp(masked_scores(query_row, key_row, ids_row) - log_total[..., None])
    grad_probs = jnp.einsum(
        "thd,uhd->htu", grad_context, value_row, preferred_element_type=jnp.float32
    )
    value_grad = jnp.einsum(
        "htu,thd->uhd", probs.astype(jnp.bfloat16), grad_context, preferred_element_type=jnp.float32
    )
    row_delta = jnp.sum(grad_probs * probs, axis=-1, keepdims=True)
    grad_scores = (probs * (grad_probs - row_delta)).astype(jnp.bfloat16)
    query_grad = score_scale * jnp.einsum(
        "htu,uhd->thd", grad_scores, key_row, preferred_element_type=jnp.float32
    )
    key_grad = score_scale * jnp.einsum(
        "htu,thd->uhd", grad_scores, query_row, preferred_element_type=jnp.float32
    )
    return (query_grad, key_grad, value_grad)


def body(
    tokens,
    segment_ids,
    cotangent,
    w_proj,
    w_point,
    w_out,
    w_up,
    w_down,
    proj_bias,
    conv_depth,
    kernel_weight,
    kernel_bias,
    hidden_bias,
    up_bias,
    norm_gain,
):
    row_count, seq_length = segment_ids.shape
    half_width = KERNEL // 2
    head_shape = (row_count, seq_length, HEADS, HEAD_DIM)
    group_in = (row_count, seq_length, GROUPS, D // GROUPS)
    group_mid = (row_count, seq_length, GROUPS, FF // GROUPS)
    gathered = (
        lax.all_gather(w_proj.astype(jnp.bfloat16), ("dp", "fsdp"), axis=0, tiled=True),
        lax.all_gather(w_point.astype(jnp.bfloat16), ("dp", "fsdp"), axis=0, tiled=True),
        lax.all_gather(w_out.astype(jnp.bfloat16), ("dp", "fsdp"), axis=0, tiled=True),
        lax.all_gather(w_up.astype(jnp.bfloat16), ("dp", "fsdp"), axis=2, tiled=True),
        lax.all_gather(w_down.astype(jnp.bfloat16), ("dp", "fsdp"), axis=1, tiled=True),
    )
    proj_full, point_full, out_full, up_full, down_full = gathered
    tap_valid = tap_mask(segment_ids)
    inputs = tokens.astype(jnp.float32)
    projected = jnp.einsum("rsd,de->rse", tokens, proj_full, preferred_element_type=jnp.float32)
    queries = (projected[..., :ATT] + proj_bias[0]).astype(jnp.bfloat16)
    key_heads = projected[..., ATT : 2 * ATT].astype(jnp.bfloat16)
    value_heads = (projected[..., 2 * ATT : 3 * ATT] + proj_bias[1]).astype(jnp.bfloat16)
    conv_input = projected[..., 3 * ATT :] + proj_bias[2]
    depth_out = jnp.zeros_like(inputs)
    for tap_index in range(KERNEL):
        depth_out = depth_out + conv_depth[tap_index] * tap_valid[
            ..., tap_index : tap_index + 1
        ] * shifted(inputs, tap_index - half_width)
    depth_low = depth_out.astype(jnp.bfloat16)
    key_conv = (
        jnp.einsum("rsd,de->rse", depth_low, point_full, preferred_element_type=jnp.float32)
        + proj_bias[3]
    )
    query_float = queries.astype(jnp.float32)
    conv_attn = key_conv * query_float
    kernel_logits = (
        jnp.einsum("rse,ek->rsk", conv_attn, kernel_weight, precision=precise) + kernel_bias
    )
    kernel_soft = jax.nn.softmax(
        kernel_logits.reshape(row_count, seq_length, HEADS, KERNEL), axis=-1
    )
    kernel_masked = kernel_soft * tap_valid[:, :, None, :]
    conv_heads = conv_input.reshape(head_shape)
    conv_out = jnp.zeros_like(conv_heads)
    for tap_index in range(KERNEL):
        conv_out = conv_out + kernel_masked[..., tap_index : tap_index + 1] * shifted(
            conv_heads, tap_index - half_width
        )
    query_heads = queries.reshape(head_shape)
    key_split = key_heads.reshape(head_shape)
    value_split = value_heads.reshape(head_shape)
    context, log_totals = lax.map(attend_row, (query_heads, key_split, value_split, segment_ids))
    mixed = jnp.concatenate(
        [context.reshape(row_count, seq_length, ATT), conv_out.reshape(row_count, seq_length, ATT)],
        axis=-1,
    ).astype(jnp.bfloat16)
    attended = (
        jnp.einsum("rse,ed->rsd", mixed, out_full, preferred_element_type=jnp.float32)
        + hidden_bias[0]
    )
    first_norm, normed_one, inv_one = norm_forward(attended + inputs, norm_gain[0], hidden_bias[1])
    first_low = first_norm.astype(jnp.bfloat16).reshape(group_in)
    raised = (
        jnp.einsum(
            "rsgi,gij->rsgj", first_low, up_full, preferred_element_type=jnp.float32
        ).reshape(row_count, seq_length, FF)
        + up_bias
    )
    activated, gelu_pull = jax.vjp(gelu_exact, raised)
    act_low = activated.astype(jnp.bfloat16).reshape(group_mid)
    lowered = (
        jnp.einsum(
            "rsgj,gji->rsgi", act_low, down_full, preferred_element_type=jnp.float32
        ).reshape(row_count, seq_length, D)
        + hidden_bias[2]
    )
    layer_out, normed_two, inv_two = norm_forward(
        lowered + first_norm, norm_gain[1], hidden_bias[3]
    )
    back_weights = (
        lax.all_gather(w_proj.astype(jnp.bfloat16), ("dp", "fsdp"), axis=0, tiled=True),
        lax.all_gather(w_point.astype(jnp.bfloat16), ("dp", "fsdp"), axis=0, tiled=True),
        lax.all_gather(w_out.astype(jnp.bfloat16), ("dp", "fsdp"), axis=0, tiled=True),
        lax.all_gather(w_up.astype(jnp.bfloat16), ("dp", "fsdp"), axis=2, tiled=True),
        lax.all_gather(w_down.astype(jnp.bfloat16), ("dp", "fsdp"), axis=1, tiled=True),
    )
    proj_back, point_back, out_back, up_back, down_back = back_weights
    grad_two, gain_two, shift_two = norm_backward(
        cotangent.astype(jnp.float32), normed_two, inv_two, norm_gain[1]
    )
    grad_lowered = grad_two.astype(jnp.bfloat16).reshape(group_in)
    down_grad = jnp.einsum(
        "rsgj,rsgi->gji", act_low, grad_lowered, preferred_element_type=jnp.float32
    )
    grad_act = jnp.einsum(
        "rsgi,gji->rsgj", grad_lowered, down_back, preferred_element_type=jnp.float32
    ).reshape(row_count, seq_length, FF)
    grad_raised = gelu_pull(grad_act)[0]
    raised_low = grad_raised.astype(jnp.bfloat16).reshape(group_mid)
    up_grad = jnp.einsum(
        "rsgi,rsgj->gij", first_low, raised_low, preferred_element_type=jnp.float32
    )
    grad_first = (
        jnp.einsum(
            "rsgj,gij->rsgi", raised_low, up_back, preferred_element_type=jnp.float32
        ).reshape(row_count, seq_length, D)
        + grad_two
    )
    grad_one, gain_one, shift_one = norm_backward(grad_first, normed_one, inv_one, norm_gain[0])
    attended_low = grad_one.astype(jnp.bfloat16)
    out_grad = jnp.einsum("rse,rsd->ed", mixed, attended_low, preferred_element_type=jnp.float32)
    grad_mixed = jnp.einsum(
        "rsd,ed->rse", attended_low, out_back, preferred_element_type=jnp.float32
    ).astype(jnp.bfloat16)
    grad_context = grad_mixed[..., :ATT].reshape(head_shape)
    grad_conv = grad_mixed[..., ATT:].astype(jnp.float32).reshape(head_shape)
    kernel_columns = []
    grad_conv_input = jnp.zeros_like(conv_heads)
    for tap_index in range(KERNEL):
        offset = tap_index - half_width
        kernel_columns.append(jnp.sum(grad_conv * shifted(conv_heads, offset), axis=-1))
        grad_conv_input = grad_conv_input + shifted(
            kernel_masked[..., tap_index : tap_index + 1] * grad_conv, -offset
        )
    grad_kernel = jnp.stack(kernel_columns, axis=-1) * tap_valid[:, :, None, :]
    grad_logits = kernel_soft * (
        grad_kernel - jnp.sum(grad_kernel * kernel_soft, axis=-1, keepdims=True)
    )
    grad_logits = grad_logits.reshape(row_count, seq_length, HEADS * KERNEL)
    kernel_bias_grad = jnp.sum(grad_logits, axis=(0, 1))
    kernel_weight_grad = jnp.einsum("rse,rsk->ek", conv_attn, grad_logits, precision=precise)
    grad_attn = jnp.einsum("rsk,ek->rse", grad_logits, kernel_weight, precision=precise)
    grad_key_conv = grad_attn * query_float
    query_from_conv = grad_attn * key_conv
    key_conv_low = grad_key_conv.astype(jnp.bfloat16)
    point_grad = jnp.einsum(
        "rsd,rse->de", depth_low, key_conv_low, preferred_element_type=jnp.float32
    )
    grad_depth = jnp.einsum(
        "rse,de->rsd", key_conv_low, point_back, preferred_element_type=jnp.float32
    )
    depth_rows = []
    tokens_grad = grad_one
    for tap_index in range(KERNEL):
        offset = tap_index - half_width
        tap_column = tap_valid[..., tap_index : tap_index + 1]
        depth_rows.append(jnp.sum(tap_column * shifted(inputs, offset) * grad_depth, axis=(0, 1)))
        tokens_grad = tokens_grad + shifted(
            conv_depth[tap_index] * tap_column * grad_depth, -offset
        )
    conv_depth_grad = jnp.stack(depth_rows, axis=0)
    query_att, key_att, value_att = lax.map(
        attend_back, (query_heads, key_split, value_split, segment_ids, log_totals, grad_context)
    )
    grad_queries = query_att.reshape(row_count, seq_length, ATT) + query_from_conv
    value_flat = value_att.reshape(row_count, seq_length, ATT)
    conv_input_flat = grad_conv_input.reshape(row_count, seq_length, ATT)
    grad_proj = jnp.concatenate(
        [grad_queries, key_att.reshape(row_count, seq_length, ATT), value_flat, conv_input_flat],
        axis=-1,
    )
    proj_bias_grad = jnp.stack(
        [
            jnp.sum(grad_queries, axis=(0, 1)),
            jnp.sum(value_flat, axis=(0, 1)),
            jnp.sum(conv_input_flat, axis=(0, 1)),
            jnp.sum(grad_key_conv, axis=(0, 1)),
        ],
        axis=0,
    )
    proj_low = grad_proj.astype(jnp.bfloat16)
    proj_grad = jnp.einsum("rsd,rse->de", tokens, proj_low, preferred_element_type=jnp.float32)
    tokens_grad = tokens_grad + jnp.einsum(
        "rse,de->rsd", proj_low, proj_back, preferred_element_type=jnp.float32
    )
    hidden_bias_grad = jnp.stack(
        [jnp.sum(grad_one, axis=(0, 1)), shift_one, jnp.sum(grad_two, axis=(0, 1)), shift_two],
        axis=0,
    )
    up_bias_grad = jnp.sum(grad_raised, axis=(0, 1))
    norm_gain_grad = jnp.stack([gain_one, gain_two], axis=0)
    matrix_shares = (
        lax.psum_scatter(proj_grad, ("dp", "fsdp"), scatter_dimension=0, tiled=True),
        lax.psum_scatter(point_grad, ("dp", "fsdp"), scatter_dimension=0, tiled=True),
        lax.psum_scatter(out_grad, ("dp", "fsdp"), scatter_dimension=0, tiled=True),
        lax.psum_scatter(up_grad, ("dp", "fsdp"), scatter_dimension=2, tiled=True),
        lax.psum_scatter(down_grad, ("dp", "fsdp"), scatter_dimension=1, tiled=True),
    )
    small_sums = lax.psum(
        (
            proj_bias_grad,
            conv_depth_grad,
            kernel_weight_grad,
            kernel_bias_grad,
            hidden_bias_grad,
            up_bias_grad,
            norm_gain_grad,
        ),
        ("dp", "fsdp"),
    )
    return (
        layer_out.astype(jnp.bfloat16),
        tokens_grad,
        matrix_shares[0],
        matrix_shares[1],
        matrix_shares[2],
        matrix_shares[3],
        matrix_shares[4],
        small_sums[0],
        small_sums[1],
        small_sums[2],
        small_sums[3],
        small_sums[4],
        small_sums[5],
        small_sums[6],
    )


def solution(mesh):
    placed = (
        P(("dp", "fsdp"), None, None),
        P(("dp", "fsdp"), None),
        P(("dp", "fsdp"), None, None),
        P(("dp", "fsdp"), None),
        P(("dp", "fsdp"), None),
        P(("dp", "fsdp"), None),
        P(None, None, ("dp", "fsdp")),
        P(None, ("dp", "fsdp"), None),
        P(),
        P(),
        P(),
        P(),
        P(),
        P(),
        P(),
    )
    return jax.shard_map(
        body,
        mesh=mesh,
        in_specs=placed,
        out_specs=(
            P(("dp", "fsdp"), None, None),
            P(("dp", "fsdp"), None, None),
            P(("dp", "fsdp"), None),
            P(("dp", "fsdp"), None),
            P(("dp", "fsdp"), None),
            P(None, None, ("dp", "fsdp")),
            P(None, ("dp", "fsdp"), None),
            P(),
            P(),
            P(),
            P(),
            P(),
            P(),
            P(),
        ),
        check_vma=False,
    )
```

profile of v0, /device:TPU:0, one launch (start us, length us, event | category | flops | bytes accessed | tf_op | source)
XLA Modules:
  0.0 1151.4 jit_solution(13410784624799127255)
XLA Ops:
  27.5 45.2 %all_gather.21 = bf16[768,384]{1,0:T(8,128)(2,1)S(1)} all-gather(bf16[24,384]{1,0:T(8,128)(2,1)S(1)} %convert_element_type.146), channel_id=1, replica_groups=mesh['dp'=16,'fsdp'=2] {'dp','fsdp'}, dimensions={0}, use_global_device_ids=true | all-gather | bytes 608256 | tf_op jit(solution)/shard_map/all_gather | solution.py:128
  77.2 10.2 fusion.98
  89.0 3.5 fusion.156
  92.5 6.7 fusion.136
  108.4 5.4 fusion.150
  121.9 34.6 %while.28 = (s32[]{:T(128)}, bf16[4,512,6,64]{1,3,2,0:T(8,128)(2,1)}, f32[4,6,512]{2,1,0:T(8,128)}, bf16[4,512,6,64]{1,3,2,0:T(8,128)(2,1)}, s32[4,512]{1,0:T(4,...) while((s32[]{:T(128)}, bf16[4,512,6,64]{1,3,2,0:T(8,128)(2,1)}, ...), condition=%wide.region_3.4_spmd.clone, body=%wide.region_0.0_spmd.sunk.clone | while | flops 421786624 | bytes 34590868 | solution.py:169
  159.6 3.6 copy.125
  163.2 19.2 %add_convert_fusion.1 = bf16[4,512,6,64]{1,3,2,0:T(8,128)(2,1)S(1)} fusion(f32[4,512,6,64]{1,3,2,0:T(8,128)} %bitcast.380, f32[4,512,6]{1,2,0:T(8,128)S(1)} %copy.133, f32[4,512,6]{1,2,0:T(8,128)S(1)} %copy.132, f32[4,512,6]{1,2,0:T(8,128)} %copy.131, f32[4,512,6]{1,2,0:T(8,128)} %copy.130, f32[4,512,6]{1,2,0:T(8,128)S(1)} %copy.129, ...), kind=kLoop, calls=%fused_computation.232 | loop fusion | flops 14155776 | bytes 5160960 | tf_op jit(solution)/shard_map/convert.10
  183.3 6.4 fusion.192
  193.6 61.6 %fusion.61 = (bf16[4,512,2,1536]{3,1,0,2:T(8,128)(2,1)}, f32[4,512,2,1536]{3,1,0,2:T(8,128)}, f32[2,4,512,1536]{3,2,1,0:T(8,128)}) fusion(f32[2,1536]{1,0:T(2,128)S(1)} %add.353, bf16[2,384,1536]{1,2,0:T(8,128)(2,1)} %all-gather.9.cloned.1.call-done, bf16[4,64,2,8,384]{4,3,2,1,0:T(8,128)(2,1)S(1)} %bitcast.394), kind=kOutput, calls=%fused_computation.78 | convolution fusion | flops 5247074304 | bytes 68431872 | tf_op jit(solution)/shard_map/rsgi,gij->rsgj/dot_general | solution.py:181
  255.3 10.7 convolution_bitcast_fusion.2
  266.0 10.3 copy.137
  276.4 9.1 reshape.337
  285.4 5.7 fusion.187
  292.0 3.3 copy-done.8
  299.5 26.4 %fusion.193 = (f32[2,1536]{1,0:T(2,128)}, bf16[4,512,2,1536]{3,1,0,2:T(8,128)(2,1)}) fusion(f32[4,512,2,1536]{3,1,0,2:T(8,128)} %get-tuple-element.268, bf16[2,1536,384]{2,1,0:T(8,128)(2,1)} %all-gather.11.cloned.1.call-done, bf16[4,64,2,8,384]{4,3,2,1,0:T(8,128)(2,1)S(1)} %bitcast.396, f32[2,4,512,1536]{3,2,1,0:T(8,128)} %get-tuple-element.325, ...), kind=kOutput, calls=%fused_computation.387 | convolution fusion | flops 4932498432 | bytes 68444160 | tf_op jit(solution)/shard_map/rsgi,gji->rsgj/dot_general | solution.py:212
  325.9 10.7 fusion.127
  336.7 10.3 copy.139
  347.0 9.2 reshape.339
  356.2 12.0 %fusion.99 = (f32[768]{0:T(1024)S(1)}, f32[768]{0:T(1024)S(1)}, f32[768]{0:T(1024)S(1)}, f32[768]{0:T(1024)S(1)}, f32[4,512]{1,0:T(4,128)S(1)}, /*index=5*/f32[4...) fusion(bf16[4,512,768]{2,1,0:T(8,128)(2,1)} %param.21, ...), kind=kLoop, calls=%fused_computation.146 | loop fusion | flops 39313664 | bytes 31547392 | tf_op jit(solution)/shard_map/reduce_sum | solution.py:55
  376.9 68.1 %while.29 = (s32[]{:T(128)}, f32[4,512,6,64]{1,3,2,0:T(8,128)}, bf16[4,512,6,64]{1,3,2,0:T(8,128)(2,1)}, f32[4,512,6,64]{1,3,2,0:T(8,128)}, bf16[4,512,6,64]{1,3...) while((s32[]{:T(128)}, f32[4,512,6,64]{1,3,2,0:T(8,128)}, ...), condition=%wide.region_26.27_spmd.clone, body=%wide.region_24.26_spmd.sunk.clone | while | flops 1030878208 | bytes 53443700 | solution.py:269
  381.0 3.7 fusion.253
  384.7 3.3 multiply_reduce_fusion.27
  397.9 3.7 fusion.253
  414.9 3.6 fusion.253
  418.5 3.3 multiply_reduce_fusion.27
  431.8 3.7 fusion.253
  445.1 3.7 copy.163
  448.8 3.5 copy.142
  452.3 16.6 %multiply_reduce_fusion.15 = (f32[4,512,6]{1,2,0:T(8,128)S(1)}, f32[4,512,6]{1,2,0:T(8,128)S(1)}, f32[4,512,6]{1,2,0:T(8,128)S(1)}, f32[4,512,6]{1,2,0:T(8,128)S...) fusion(f32[4,512,6,64]{1,3,2,0:T(8,128)} %bitcast.382, ...), kind=kLoop, calls=%fused_computation.223 | loop fusion | flops 20336640 | bytes 32292864 | tf_op jit(solution)/shard_map/reduce_sum | solution.py:238
  474.1 6.9 fusion.183
  481.1 5.9 convolution_bitcast_fusion.3
  487.1 7.5 fusion.145
  494.7 12.5 %convolution_bitcast_fusion = f32[2,1536,384]{2,1,0:T(8,128)} fusion(bf16[4,512,2,1536]{3,1,0,2:T(8,128)(2,1)} %get-tuple-element.267, bf16[4,64,2,8,384]{4,3,2,1,0:T(8,128)(2,1)} %bitcast.397), kind=kOutput, calls=%fused_computation.199 | convolution fusion | flops 4831838208 | bytes 20447232 | tf_op jit(solution)/shard_map/rsgj,rsgi->gji/dot_general | solution.py:209
  507.2 11.2 fusion.105
  518.6 4.6 fusion.189
  528.7 12.5 %fusion.184 = (f32[6,64]{1,0:T(8,128)S(1)}, bf16[4,512,6,64]{1,3,2,0:T(8,128)(2,1)}) fusion(f32[4,512,6,64]{1,3,2,0:T(8,128)} %get-tuple-element.304, f32[4,512,6,64]{1,3,2,0:T(8,128)} %get-tuple-element.303, f32[4,512,6,64]{1,3,2,0:T(8,128)} %get-tuple-element.302, f32[4,512,6,64]{1,3,2,0:T(8,128)} %get-tuple-element.301, ...), kind=kLoop, calls=%fused_computation.381 | loop fusion | flops 8650368 | bytes 29935104 | tf_op jit(solution)/shard_map/reduce_sum | solution.py:283
  543.2 11.2 convolution_bitcast_fusion.1
  554.6 6.2 copy.206
  561.0 22.5 %multiply_multiply_fusion = (f32[4,512,768]{2,1,0:T(8,128)}, f32[4,512,768]{2,1,0:T(8,128)}, f32[4,512,768]{2,1,0:T(8,128)}, f32[4,512,768]{2,1,0:T(8,128)}, f32...) fusion(f32[4,512]{1,0:T(4,128)S(1)} %copy-done.52, ...), kind=kOutput, calls=%fused_computation.95 | convolution fusion | flops 1235484672 | bytes 62021632 | tf_op jit(solution)/shard_map/rse,de->rsd/dot_general | solution.py:256
  583.6 13.8 %multiply_reduce_fusion.2 = (f32[768]{0:T(1024)S(1)}, f32[768]{0:T(1024)S(1)}, f32[768]{0:T(1024)S(1)}, f32[768]{0:T(1024)S(1)}, f32[768]{0:T(1024)S(1)}, /*inde...) fusion(f32[4,512,768]{2,1,0:T(8,128)} %get-tuple-element.326, ...), kind=kLoop, calls=%fused_computation.149 | loop fusion | flops 44033280 | bytes 15830016 | tf_op jit(solution)/shard_map/reduce_sum | solution.py:264
  597.6 38.9 %all-reduce.20 = (f32[4,384]{1,0:T(4,128)}, f32[9,768]{1,0:T(8,128)}, f32[54]{0:T(128)}, f32[4,768]{1,0:T(4,128)}, f32[3072]{0:T(1024)}, /*index=5*/f32[2,768]{1,0:T(2,128)}) all-reduce(f32[4,384]{1,0:T(4,128)S(1)} %pad_maximum_fusion.9, f32[9,768]{1,0:T(8,128)S(1)} %stack.163, ...), channel_id=1, replica_groups=mesh['dp'=16,'fsdp'=2] {'dp','fsdp'}, use_global_device_ids=true, to_apply=%region_36.37 | all-reduce | flops 16182 | bytes 129456 | tf_op jit(solution)/shard_map/psum | solution.py:306
  636.5 27.1 %fusion.86 = f32[4,512,768]{2,1,0:T(8,128)} fusion(f32[4,512,768]{2,1,0:T(8,128)} %copy-done.18, f32[4,512,768]{2,1,0:T(8,128)} %get-tuple-element.289, f32[4,512,768]{2,1,0:T(8,128)} %get-tuple-element.288, f32[4,512,768]{2,1,0:T(8,128)} %get-tuple-element.287, f32[4,512,768]{2,1,0:T(8,128)} %get-tuple-element.286, ...), kind=kOutput, calls=%fused_computation.133 | convolution fusion | flops 4875878400 | bytes 77868032 | tf_op jit(solution)/shard_map/rse,de->rsd/dot_general | solution.py:290
  663.7 36.8 %reduce-scatter.18.cloned.1.call-done = f32[24,384]{1,0:T(8,128)} async-done(((f32[768,384]{1,0:T(8,128)}), f32[24,384]{1,0:T(8,128)}) %reduce-scatter.18.cloned.1.call-update) | async-done | bytes 36880
  700.5 103.9 %reduce-scatter.10.cloned.1.call-done = f32[24,768]{1,0:T(8,128)} async-done(((f32[768,768]{1,0:T(8,128)}), f32[24,768]{1,0:T(8,128)}) %reduce-scatter.10.cloned.1.call-update) | async-done | bytes 73744 | tf_op jit(solution)/shard_map/reduce_scatter | solution.py:302
  804.4 113.1 %reduce-scatter.14.cloned.1.call-done = f32[2,48,384]{2,1,0:T(8,128)} async-done(((f32[2,1536,384]{2,1,0:T(8,128)}), f32[2,48,384]{2,1,0:T(8,128)}) %reduce-scatter.14.cloned.1.call-update) | async-done | bytes 147472 | tf_op jit(solution)/shard_map/reduce_scatter | solution.py:304
  917.5 112.2 %reduce-scatter.12.cloned.1.call-done = f32[2,384,48]{1,2,0:T(8,128)} async-done(((f32[2,384,1536]{1,2,0:T(8,128)}), f32[2,384,48]{1,2,0:T(8,128)}) %reduce-scatter.12.cloned.1.call-update) | async-done | bytes 147472 | tf_op jit(solution)/shard_map/reduce_scatter | solution.py:303
  1029.7 112.9 %reduce-scatter.16.cloned.1.call-done = f32[24,1536]{1,0:T(8,128)} async-done(((f32[768,1536]{1,0:T(8,128)}), f32[24,1536]{1,0:T(8,128)}) %reduce-scatter.16.cloned.1.call-update) | async-done | bytes 147472
  (401 shorter events, 160.1 us)
Async XLA Ops:
  7.2 101.2 %copy-start = (f32[384,54]{0,1:T(8,128)S(1)}, f32[384,54]{0,1:T(8,128)}, u32[]{:S(2)}) copy-start(f32[384,54]{0,1:T(8,128)} %param.29) | copy-start | bytes 248836
  7.2 85.3 %all-gather.5.cloned.1.call-start = ((), (), s32[]{:S(2)}) async-start(), calls=%async_computation.5 | async-start | bytes 2433024 | tf_op jit(solution)/shard_map/all_gather | solution.py:127
  8.8 174.5 %all-gather.7.cloned.1.call-start = ((), (), s32[]{:S(2)}) async-start(), calls=%async_computation.6 | async-start | bytes 1216512 | tf_op jit(solution)/shard_map/all_gather | solution.py:129
  10.4 183.2 %all-gather.9.cloned.1.call-start = ((), (), s32[]{:S(2)}) async-start(), calls=%async_computation.7 | async-start | bytes 2433024 | tf_op jit(solution)/shard_map/all_gather | solution.py:130
  12.0 243.2 %all-gather.11.cloned.1.call-start = ((), (), s32[]{:S(2)}) async-start(), calls=%async_computation.8 | async-start | bytes 2433024 | tf_op jit(solution)/shard_map/all_gather | solution.py:131
  13.7 650.0 %all-reduce.23.cloned.1.call-start = ((), (), s32[]{:S(2)}) async-start(), calls=%async_computation.12 | async-start | bytes 172032 | tf_op jit(solution)/shard_map/psum | solution.py:306
  13.9 60.5 %copy-start.12 = (bf16[4,512,6,64]{1,3,2,0:T(8,128)(2,1)}, bf16[4,512,6,64]{1,3,2,0:T(8,128)(2,1)S(1)}, u32[]{:S(2)}) copy-start(bf16[4,512,6,64]{1,3,2,0:T(8,128)(2,1)S(1)} %fusion.191) | copy-start | bytes 4718596
  14.8 93.6 %copy-start.88 = (f32[384]{0:T(512)}, f32[384]{0:T(512)S(1)}, u32[]{:S(2)}) copy-start(f32[384]{0:T(512)S(1)} %get-tuple-element.215) | copy-start | bytes 4612
  16.2 174.3 %copy-start.65 = (f32[768]{0:T(1024)}, f32[768]{0:T(1024)S(1)}, u32[]{:S(2)}) copy-start(f32[768]{0:T(1024)S(1)} %get-tuple-element.211) | copy-start | bytes 9220
  17.0 56.9 %copy-start.13 = (bf16[4,512,768]{2,1,0:T(8,128)(2,1)S(1)}, bf16[4,512,768]{2,1,0:T(8,128)(2,1)}, u32[]{:S(2)}) copy-start(bf16[4,512,768]{2,1,0:T(8,128)(2,1)} %param.19) | copy-start | bytes 9437188
  18.5 172.1 %copy-start.86 = (f32[768]{0:T(1024)}, f32[768]{0:T(1024)S(1)}, u32[]{:S(2)}) copy-start(f32[768]{0:T(1024)S(1)} %get-tuple-element.207) | copy-start | bytes 9220
  27.2 47.2 %copy-start.70 = (f32[768]{0:T(1024)}, f32[768]{0:T(1024)S(1)}, u32[]{:S(2)}) copy-start(f32[768]{0:T(1024)S(1)} %get-tuple-element.197) | copy-start | bytes 9220
  27.2 47.2 %copy-start.72 = (f32[768]{0:T(1024)}, f32[768]{0:T(1024)S(1)}, u32[]{:S(2)}) copy-start(f32[768]{0:T(1024)S(1)} %get-tuple-element.198) | copy-start | bytes 9220
  27.2 47.2 %copy-start.74 = (f32[768]{0:T(1024)}, f32[768]{0:T(1024)S(1)}, u32[]{:S(2)}) copy-start(f32[768]{0:T(1024)S(1)} %get-tuple-element.199) | copy-start | bytes 9220
  27.3 47.2 %copy-start.76 = (f32[768]{0:T(1024)}, f32[768]{0:T(1024)S(1)}, u32[]{:S(2)}) copy-start(f32[768]{0:T(1024)S(1)} %get-tuple-element.201) | copy-start | bytes 9220
  27.3 47.2 %copy-start.78 = (f32[768]{0:T(1024)}, f32[768]{0:T(1024)S(1)}, u32[]{:S(2)}) copy-start(f32[768]{0:T(1024)S(1)} %get-tuple-element.202) | copy-start | bytes 9220
  27.3 47.2 %copy-start.80 = (f32[768]{0:T(1024)}, f32[768]{0:T(1024)S(1)}, u32[]{:S(2)}) copy-start(f32[768]{0:T(1024)S(1)} %get-tuple-element.203) | copy-start | bytes 9220
  27.3 47.2 %copy-start.82 = (f32[768]{0:T(1024)}, f32[768]{0:T(1024)S(1)}, u32[]{:S(2)}) copy-start(f32[768]{0:T(1024)S(1)} %get-tuple-element.204) | copy-start | bytes 9220
  27.3 47.2 %copy-start.84 = (f32[768]{0:T(1024)}, f32[768]{0:T(1024)S(1)}, u32[]{:S(2)}) copy-start(f32[768]{0:T(1024)S(1)} %get-tuple-element.205) | copy-start | bytes 9220
  27.3 47.2 %copy-start.90 = (f32[768]{0:T(1024)}, f32[768]{0:T(1024)S(1)}, u32[]{:S(2)}) copy-start(f32[768]{0:T(1024)S(1)} %get-tuple-element.200) | copy-start | bytes 9220
  27.3 89.9 %copy-start.27 = (f32[4,512,9]{1,0,2:T(4,128)}, f32[4,512,9]{1,0,2:T(4,128)S(1)}, u32[]{:S(2)}) copy-start(f32[4,512,9]{1,0,2:T(4,128)S(1)} %convert_element_type.143) | copy-start | bytes 221188
  27.4 47.1 %copy-start.49 = (f32[4,512]{1,0:T(4,128)}, f32[4,512]{1,0:T(4,128)S(1)}, u32[]{:S(2)}) copy-start(f32[4,512]{1,0:T(4,128)S(1)} %get-tuple-element.314) | copy-start | bytes 24580
  27.4 47.1 %copy-start.51 = (f32[4,512]{1,0:T(4,128)}, f32[4,512]{1,0:T(4,128)S(1)}, u32[]{:S(2)}) copy-start(f32[4,512]{1,0:T(4,128)S(1)} %get-tuple-element.315) | copy-start | bytes 24580
  27.4 47.1 %copy-start.53 = (f32[4,512]{1,0:T(4,128)}, f32[4,512]{1,0:T(4,128)S(1)}, u32[]{:S(2)}) copy-start(f32[4,512]{1,0:T(4,128)S(1)} %get-tuple-element.316) | copy-start | bytes 24580
  27.4 47.1 %copy-start.55 = (f32[4,512]{1,0:T(4,128)}, f32[4,512]{1,0:T(4,128)S(1)}, u32[]{:S(2)}) copy-start(f32[4,512]{1,0:T(4,128)S(1)} %get-tuple-element.317) | copy-start | bytes 24580
  27.4 47.1 %copy-start.57 = (f32[4,512]{1,0:T(4,128)}, f32[4,512]{1,0:T(4,128)S(1)}, u32[]{:S(2)}) copy-start(f32[4,512]{1,0:T(4,128)S(1)} %get-tuple-element.318) | copy-start | bytes 24580
  27.4 47.1 %copy-start.59 = (f32[4,512]{1,0:T(4,128)}, f32[4,512]{1,0:T(4,128)S(1)}, u32[]{:S(2)}) copy-start(f32[4,512]{1,0:T(4,128)S(1)} %get-tuple-element.320) | copy-start | bytes 24580
  27.4 47.1 %copy-start.61 = (f32[4,512]{1,0:T(4,128)}, f32[4,512]{1,0:T(4,128)S(1)}, u32[]{:S(2)}) copy-start(f32[4,512]{1,0:T(4,128)S(1)} %get-tuple-element.321) | copy-start | bytes 24580
  27.4 47.1 %copy-start.63 = (f32[4,512]{1,0:T(4,128)}, f32[4,512]{1,0:T(4,128)S(1)}, u32[]{:S(2)}) copy-start(f32[4,512]{1,0:T(4,128)S(1)} %get-tuple-element.322) | copy-start | bytes 24580
  27.5 47.1 %copy-start.67 = (f32[4,512]{1,0:T(4,128)}, f32[4,512]{1,0:T(4,128)S(1)}, u32[]{:S(2)}) copy-start(f32[4,512]{1,0:T(4,128)S(1)} %get-tuple-element.319) | copy-start | bytes 24580
  118.6 44.6 %copy-start.38 = (f32[4,512,6]{1,2,0:T(8,128)}, f32[4,512,6]{1,2,0:T(8,128)S(1)}, u32[]{:S(2)}) copy-start(f32[4,512,6]{1,2,0:T(8,128)S(1)} %copy.124) | copy-start | bytes 147460
  118.6 44.6 %copy-start.40 = (f32[4,512,6]{1,2,0:T(8,128)}, f32[4,512,6]{1,2,0:T(8,128)S(1)}, u32[]{:S(2)}) copy-start(f32[4,512,6]{1,2,0:T(8,128)S(1)} %copy.133) | copy-start | bytes 147460
  118.6 44.5 %copy-start.42 = (f32[4,512,6]{1,2,0:T(8,128)}, f32[4,512,6]{1,2,0:T(8,128)S(1)}, u32[]{:S(2)}) copy-start(f32[4,512,6]{1,2,0:T(8,128)S(1)} %copy.132) | copy-start | bytes 147460
  120.0 43.2 %copy-start.36 = (f32[4,512,6]{1,2,0:T(8,128)}, f32[4,512,6]{1,2,0:T(8,128)S(1)}, u32[]{:S(2)}) copy-start(f32[4,512,6]{1,2,0:T(8,128)S(1)} %copy.129) | copy-start | bytes 147460
  156.5 25.9 %copy-start.6 = (bf16[4,512,6,64]{1,3,2,0:T(8,128)(2,1)}, bf16[4,512,6,64]{1,3,2,0:T(8,128)(2,1)S(1)}, u32[]{:S(2)}) copy-start(bf16[4,512,6,64]{1,3,2,0:T(8,128)(2,1)S(1)} %get-tuple-element.569) | copy-start | bytes 4718596
  193.6 61.7 %copy-start.22 = (bf16[4,512,768]{2,1,0:T(8,128)(2,1)}, bf16[4,512,768]{2,1,0:T(8,128)(2,1)S(1)}, u32[]{:S(2)}) copy-start(bf16[4,512,768]{2,1,0:T(8,128)(2,1)S(1)} %fusion.104) | copy-start | bytes 9437188
  299.5 26.5 %copy-start.24 = (bf16[4,512,768]{2,1,0:T(8,128)(2,1)}, bf16[4,512,768]{2,1,0:T(8,128)(2,1)S(1)}, u32[]{:S(2)}) copy-start(bf16[4,512,768]{2,1,0:T(8,128)(2,1)S(1)} %fusion.180) | copy-start | bytes 9437188
  347.0 21.2 %slice-start = ((s8[6291456]{0:T(1024)(128)(4,1)}), s8[2097152]{0:T(1024)(128)(4,1)S(1)}, s32[]{:S(2)}) async-start(s8[6291456]{0:T(1024)(128)(4,1)} %bitcast.375), calls=%async_computation.15 | async-start | bytes 4194304
  452.3 17.6 %copy-start.20 = (f32[4,512,54]{1,2,0:T(8,128)S(1)}, f32[4,512,54]{1,2,0:T(8,128)}, u32[]{:S(2)}) copy-start(f32[4,512,54]{1,2,0:T(8,128)} %copy-done.19) | copy-start | bytes 1327108
  481.1 219.4 %reduce-scatter.18.cloned.1.call-start = ((), (), s32[]{:S(2)}) async-start(), calls=%async_computation.14 | async-start | bytes 1216512
  487.0 317.3 %reduce-scatter.10.cloned.1.call-start = ((), (), s32[]{:S(2)}) async-start(), calls=%async_computation.9 | async-start | bytes 2433024 | tf_op jit(solution)/shard_map/reduce_scatter | solution.py:302
  494.6 422.9 %reduce-scatter.14.cloned.1.call-start = ((), (), s32[]{:S(2)}) async-start(), calls=%async_computation.11 | async-start | bytes 4866048 | tf_op jit(solution)/shard_map/reduce_scatter | solution.py:304
  507.2 522.5 %reduce-scatter.12.cloned.1.call-start = ((), (), s32[]{:S(2)}) async-start(), calls=%async_computation.10 | async-start | bytes 4866048 | tf_op jit(solution)/shard_map/reduce_scatter | solution.py:303
  518.5 624.1 %reduce-scatter.16.cloned.1.call-start = ((), (), s32[]{:S(2)}) async-start(), calls=%async_computation.13 | async-start | bytes 4866048
  560.8 22.8 %slice-start.2 = ((s8[6291456]{0:T(1024)(128)(4,1)}), s8[2097152]{0:T(1024)(128)(4,1)S(1)}, s32[]{:S(2)}) async-start(s8[6291456]{0:T(1024)(128)(4,1)} %bitcast.377), calls=%async_computation.17 | async-start | bytes 4194304
  561.0 22.6 %slice-start.3 = ((s8[6291456]{0:T(1024)(128)(4,1)}), s8[4194304]{0:T(1024)(128)(4,1)S(1)}, s32[]{:S(2)}) async-start(s8[6291456]{0:T(1024)(128)(4,1)} %bitcast.377), calls=%async_computation.18 | async-start | bytes 8388608
  561.0 22.6 %copy-start.68 = (f32[4,512]{1,0:T(4,128)S(1)}, f32[4,512]{1,0:T(4,128)}, u32[]{:S(2)}) copy-start(f32[4,512]{1,0:T(4,128)} %copy-done.67) | copy-start | bytes 24580
  583.6 52.9 %copy-start.91 = (f32[768]{0:T(1024)S(1)}, f32[768]{0:T(1024)}, u32[]{:S(2)}) copy-start(f32[768]{0:T(1024)} %copy-done.90) | copy-start | bytes 9220
  (69 other events, 466.5 us)
Sparse Core Ops, SparseCore 0:
  11.5 60.6 all-gather.4
  75.6 53.0 all-gather.6
  132.2 56.1 all-gather.8
  191.8 56.1 all-gather.10
  481.2 115.5 all-reduce.22
  602.3 98.1 reduce-scatter.17
  706.4 97.9 reduce-scatter.9
  811.3 106.0 reduce-scatter.13
  923.5 106.1 reduce-scatter.11
  1036.5 106.0 reduce-scatter.15
where the time goes:
time: 1160 us; the launch traced here: 1150 us
  waiting for transfers between devices  479 us (41%)
  matrix products  316 us (27%)
  other arithmetic  144 us (12%)
  local copies, waits for them, and re-layouts  110 us (9%)
  blocking collectives  84.1 us (7%)
  between operations  16.4 us (1%)
    unnamed x12, waiting for transfers between devices  150 us
    reduce_scatter x1, waiting for transfers between devices, body(): lax.psum_scatter(down_grad, ('dp', 'fsdp'), scatter_dimension=1, tiled=True)  113 us
    reduce_scatter x1, waiting for transfers between devices, body(): lax.psum_scatter(up_grad, ('dp', 'fsdp'), scatter_dimension=2, tiled=True)  112 us
    reduce_scatter x1, waiting for transfers between devices, body(): lax.psum_scatter(out_grad, ('dp', 'fsdp'), scatter_dimension=0, tiled=True)  104 us
    dot_general x1, matrix products, body(): jnp.einsum('rsgi,gij->rsgj', first_low, up_full, preferred_element_type=j...  61.6 us
    all_gather x1, blocking collectives, body(): lax.all_gather(w_point.astype(jnp.bfloat16), ('dp', 'fsdp'), axis=0, tile...  45.2 us
    psum x1, blocking collectives, body(): lax.psum((proj_bias_grad, conv_depth_grad, kernel_weight_grad, kernel_bia...  38.9 us
    dot_general x1, matrix products, body(): jnp.einsum('rse,de->rsd', proj_low, proj_back, preferred_element_type=jnp...  27.1 us
  transfers between devices with their start and end apart: 10, of which 5 were waited for; matrix products, arithmetic and copies ran while one was open for 29% of the time, Pallas kernels for 0%

commit v1 on v0

--- a/solution.py
+++ b/solution.py
@@ -1,3 +1,4 @@
+import functools
 import jax
 import jax.numpy as jnp
 from jax import lax
@@ -10,6 +11,65 @@
 KERNEL = 9
 GROUPS = 2
 ATT = 384
+
+def digits(size):
+    out, bit = [], 1
+    while bit < size:
+        ways = 4 if size // bit % 4 == 0 else 2
+        out.append((bit, ways))
+        bit *= ways
+    return out
+
+def send_xor(x, axis, size, step):
+    return lax.ppermute(x, axis, [(i, i ^ step) for i in range(size)])
+
+def gather_axis(x, axis, size):
+    x = x[None]
+    me = lax.axis_index(axis)
+    for bit, ways in reversed(digits(size)):
+        mine = (me // bit) % ways
+        got = [x] + [send_xor(x, axis, size, d * bit) for d in range(1, ways)]
+        parts = []
+        for place in range(ways):
+            rel = mine ^ place
+            part = got[0]
+            for d in range(1, ways):
+                part = jnp.where(rel == d, got[d], part)
+            parts.append(part)
+        x = jnp.stack(parts, axis=1).reshape((x.shape[0] * ways,) + x.shape[1:])
+    return x
+
+def gather_all(x, sizes):
+    nd, nf = sizes
+    g = gather_axis(x, "dp", nd)
+    g = gather_axis(g, "fsdp", nf)
+    return jnp.swapaxes(g, 0, 1)
+
+def scatter_axis(g, axis, size):
+    me = lax.axis_index(axis)
+    for bit, ways in digits(size):
+        high = g.shape[0] // ways
+        mine = (me // bit) % ways
+        h = g.reshape((high, ways) + g.shape[1:])
+        pick = lambda d: lax.dynamic_index_in_dim(h, mine ^ d, 1, keepdims=False)
+        got = [send_xor(pick(d), axis, size, d * bit) for d in range(1, ways)]
+        total = pick(0).astype(jnp.float32)
+        for r in got:
+            total = total + r.astype(jnp.float32)
+        g = total.astype(jnp.bfloat16)
+    return g[0]
+
+def scatter_all(g, sizes):
+    nd, nf = sizes
+    g = scatter_axis(jnp.swapaxes(g, 0, 1), "fsdp", nf)
+    return scatter_axis(g, "dp", nd)
+
+def sum_axis(x, axis, size):
+    for bit, ways in digits(size):
+        got = [send_xor(x, axis, size, d * bit) for d in range(1, ways)]
+        for r in got:
+            x = x + r
+    return x
 
 
 precise = lax.Precision.HIGHEST
@@ -117,20 +177,24 @@
     hidden_bias,
     up_bias,
     norm_gain,
+    *,
+    sizes,
 ):
     row_count, seq_length = segment_ids.shape
     half_width = KERNEL // 2
     head_shape = (row_count, seq_length, HEADS, HEAD_DIM)
     group_in = (row_count, seq_length, GROUPS, D // GROUPS)
     group_mid = (row_count, seq_length, GROUPS, FF // GROUPS)
-    gathered = (
-        lax.all_gather(w_proj.astype(jnp.bfloat16), ("dp", "fsdp"), axis=0, tiled=True),
-        lax.all_gather(w_point.astype(jnp.bfloat16), ("dp", "fsdp"), axis=0, tiled=True),
-        lax.all_gather(w_out.astype(jnp.bfloat16), ("dp", "fsdp"), axis=0, tiled=True),
-        lax.all_gather(w_up.astype(jnp.bfloat16), ("dp", "fsdp"), axis=2, tiled=True),
-        lax.all_gather(w_down.astype(jnp.bfloat16), ("dp", "fsdp"), axis=1, tiled=True),
-    )
-    proj_full, point_full, out_full, up_full, down_full = gathered
+    bf16 = jnp.bfloat16
+    first_shard = jnp.concatenate([w_proj, w_point], axis=1).astype(bf16)
+    first_full = gather_all(first_shard, sizes).reshape(D, 5 * ATT)
+    proj_full, point_full = first_full[:, : 4 * ATT], first_full[:, 4 * ATT :]
+    out_full = gather_all(w_out.astype(bf16), sizes).reshape(D, D)
+    ff_shard = jnp.concatenate([jnp.swapaxes(w_up, 1, 2), w_down], axis=2).astype(bf16)
+    ff_full = gather_all(ff_shard, sizes)
+    ff_full = ff_full.transpose(2, 0, 1, 3, 4).reshape(GROUPS, FF // GROUPS, D)
+    up_full = jnp.swapaxes(ff_full[..., : D // GROUPS], 1, 2)
+    down_full = ff_full[..., D // GROUPS :]
     tap_valid = tap_mask(segment_ids)
     inputs = tokens.astype(jnp.float32)
     projected = jnp.einsum("rsd,de->rse", tokens, proj_full, preferred_element_type=jnp.float32)
@@ -194,14 +258,9 @@
     layer_out, normed_two, inv_two = norm_forward(
         lowered + first_norm, norm_gain[1], hidden_bias[3]
     )
-    back_weights = (
-        lax.all_gather(w_proj.astype(jnp.bfloat16), ("dp", "fsdp"), axis=0, tiled=True),
-        lax.all_gather(w_point.astype(jnp.bfloat16), ("dp", "fsdp"), axis=0, tiled=True),
-        lax.all_gather(w_out.astype(jnp.bfloat16), ("dp", "fsdp"), axis=0, tiled=True),
-        lax.all_gather(w_up.astype(jnp.bfloat16), ("dp", "fsdp"), axis=2, tiled=True),
-        lax.all_gather(w_down.astype(jnp.bfloat16), ("dp", "fsdp"), axis=1, tiled=True),
-    )
-    proj_back, point_back, out_back, up_back, down_back = back_weights
+    proj_back, point_back, out_back, up_back, down_back = (
+        proj_full, point_full, out_full, up_full, down_full
+    )
     grad_two, gain_two, shift_two = norm_backward(
         cotangent.astype(jnp.float32), normed_two, inv_two, norm_gain[1]
     )
@@ -296,25 +355,39 @@
     )
     up_bias_grad = jnp.sum(grad_raised, axis=(0, 1))
     norm_gain_grad = jnp.stack([gain_one, gain_two], axis=0)
+    nd, nf = sizes
+    shard_rows, ff_rows = D // (nd * nf), FF // GROUPS // (nd * nf)
+    ff_grad = jnp.concatenate([jnp.swapaxes(up_grad, 1, 2), down_grad], axis=2).astype(bf16)
+    ff_grad = ff_grad.reshape(GROUPS, nd, nf, ff_rows, D).transpose(1, 2, 0, 3, 4)
+    ff_share = scatter_all(ff_grad, sizes).astype(jnp.float32)
+    out_share = scatter_all(out_grad.astype(bf16).reshape(nd, nf, shard_rows, D), sizes)
+    first_grad = jnp.concatenate([proj_grad, point_grad], axis=1).astype(bf16)
+    first_share = scatter_all(first_grad.reshape(nd, nf, shard_rows, 5 * ATT), sizes)
+    first_share = first_share.astype(jnp.float32)
     matrix_shares = (
-        lax.psum_scatter(proj_grad, ("dp", "fsdp"), scatter_dimension=0, tiled=True),
-        lax.psum_scatter(point_grad, ("dp", "fsdp"), scatter_dimension=0, tiled=True),
-        lax.psum_scatter(out_grad, ("dp", "fsdp"), scatter_dimension=0, tiled=True),
-        lax.psum_scatter(up_grad, ("dp", "fsdp"), scatter_dimension=2, tiled=True),
-        lax.psum_scatter(down_grad, ("dp", "fsdp"), scatter_dimension=1, tiled=True),
-    )
-    small_sums = lax.psum(
-        (
-            proj_bias_grad,
-            conv_depth_grad,
-            kernel_weight_grad,
-            kernel_bias_grad,
-            hidden_bias_grad,
-            up_bias_grad,
-            norm_gain_grad,
-        ),
-        ("dp", "fsdp"),
-    )
+        first_share[:, : 4 * ATT],
+        first_share[:, 4 * ATT :],
+        out_share.astype(jnp.float32),
+        jnp.swapaxes(ff_share[..., : D // GROUPS], 1, 2),
+        ff_share[..., D // GROUPS :],
+    )
+    smalls = (
+        proj_bias_grad,
+        conv_depth_grad,
+        kernel_weight_grad,
+        kernel_bias_grad,
+        hidden_bias_grad,
+        up_bias_grad,
+        norm_gain_grad,
+    )
+    flat = jnp.concatenate([small.reshape(-1) for small in smalls])
+    padded = -flat.size % 1024
+    flat = jnp.pad(flat, (0, padded)).reshape(-1, 128)
+    flat = sum_axis(sum_axis(flat, "fsdp", nf), "dp", nd).reshape(-1)
+    small_sums, at = [], 0
+    for small in smalls:
+        small_sums.append(flat[at : at + small.size].reshape(small.shape))
+        at += small.size
     return (
         layer_out.astype(jnp.bfloat16),
         tokens_grad,
@@ -352,7 +425,7 @@
         P(),
     )
     return jax.shard_map(
-        body,
+        functools.partial(body, sizes=(mesh.shape["dp"], mesh.shape["fsdp"])),
         mesh=mesh,
         in_specs=placed,
         out_specs=(

time: 1160 us -> 783 us (0.68)
  waiting for transfers between devices: 479 us -> 96.3 us
  blocking collectives: 84.1 us -> 0 us
  other arithmetic: 144 us -> 222 us
  starting transfers between devices: 0.41 us -> 61.8 us
  matrix products: 316 us -> 297 us
  local copies, waits for them, and re-layouts: 110 us -> 95.3 us
  between operations: 16.4 us -> 3.23 us
    reduce_scatter x3 -> x0, waiting for transfers between devices: 329 us -> none  [the longest x1 113 us: body(): lax.psum_scatter(down_grad, ('dp', 'fsdp'), scatter_dimension=1, tiled=True)]
    unnamed x12 -> x0, waiting for transfers between devices: 150 us -> none
    ppermute x0 -> x49, waiting for transfers between devices: none -> 96.3 us  [send_xor(): return lax.ppermute(x, axis, [(i, i ^ step) for i in range(size)])]
    ppermute x0 -> x49, starting transfers between devices: none -> 61.8 us  [send_xor(): return lax.ppermute(x, axis, [(i, i ^ step) for i in range(size)])]
    all_gather x1 -> x0, blocking collectives: 45.2 us -> none  [body(): lax.all_gather(w_point.astype(jnp.bfloat16), ('dp', 'fsdp'), axis=0, tile...]
    psum x1 -> x0, blocking collectives: 38.9 us -> none  [body(): lax.psum((proj_bias_grad, conv_depth_grad, kernel_weight_grad, kernel_bia...]
    convert_element_type x1, other arithmetic: 10.2 us -> 29.9 us  [body(): depth_low = depth_out.astype(jnp.bfloat16)]
    reduce_sum x1, other arithmetic: 13.8 us -> 30.6 us  [body(): jnp.sum(tap_column * shifted(inputs, offset) * grad_depth, axis=(0, 1))]
  transfers between devices with their start and end apart: 10 -> 49, of which waited for: 5 -> 23; matrix products, arithmetic and copies ran while one was open for 29% -> 50% of each run, Pallas kernels for 0% -> 0%
where the time goes in v1:
time: 783 us; the launch traced here: 776 us
  matrix products  297 us (38%)
  other arithmetic  222 us (28%)
  waiting for transfers between devices  96.3 us (12%)
  local copies, waits for them, and re-layouts  95.3 us (12%)
  starting transfers between devices  61.8 us (8%)
    ppermute x49, waiting for transfers between devices, send_xor(): return lax.ppermute(x, axis, [(i, i ^ step) for i in range(size)])  96.3 us
    dot_general x1, matrix products, body(): jnp.einsum('rsgi,gij->rsgj', first_low, up_full, preferred_element_type=j...  62.4 us
    ppermute x49, starting transfers between devices, send_xor(): return lax.ppermute(x, axis, [(i, i ^ step) for i in range(size)])  61.8 us
    reduce_sum x1, other arithmetic, body(): jnp.sum(tap_column * shifted(inputs, offset) * grad_depth, axis=(0, 1))  30.6 us
    convert_element_type x1, other arithmetic, body(): depth_low = depth_out.astype(jnp.bfloat16)  29.9 us
    dot_general x1, matrix products, body(): jnp.einsum('rse,de->rsd', proj_low, proj_back, preferred_element_type=jnp...  28.1 us
    dot_general x1, matrix products, body(): jnp.einsum('rsgi,gji->rsgj', grad_lowered, down_back, preferred_element_t...  26.6 us
    reduce_sum x1, other arithmetic, body(): jnp.sum(grad_conv * shifted(conv_heads, offset), axis=-1)  25.9 us
  transfers between devices with their start and end apart: 49, of which 23 were waited for; matrix products, arithmetic and copies ran while one was open for 50% of the time, Pallas kernels for 0%

profile of v1, /device:TPU:0, one launch (start us, length us, event | category | flops | bytes accessed | tf_op | source)
XLA Modules:
  0.0 776.1 jit_solution(12798260382800802834)
XLA Ops:
  26.0 5.1 convert_element_type.328
  32.4 29.9 %fusion.98 = bf16[4,512,768]{2,1,0:T(8,128)(2,1)S(1)} fusion(f32[4,512,768]{2,1,0:T(8,128)} %convert_element_type.328, f32[4,512]{1,0:T(4,128)S(1)} %get-tuple-element.340, f32[768]{0:T(1024)S(1)} %get-tuple-element.183, f32[4,512]{1,0:T(4,128)S(1)} %get-tuple-element.341, f32[768]{0:T(1024)S(1)} %get-tuple-element.184, ...), kind=kLoop, calls=%fused_computation.146 | loop fusion | flops 42467328 | bytes 9538560 | tf_op jit(solution)/shard_map/convert_element_type | solution.py:210
  67.9 3.8 collective-permute-start.1
  80.2 3.7 collective-permute-done.1
  90.8 4.5 collective-permute-done.12
  97.8 4.9 collective-permute-done.11
  105.5 10.3 %collective-permute-done.5 = bf16[4,2,48,768]{3,2,1,0:T(8,128)(2,1)S(1)} collective-permute-done((bf16[4,2,48,768]{3,2,1,0:T(8,128)(2,1)S(1)}, bf16[4,2,48,768]{3,2,1,0:T(8,128)(2,1)S(1)}, u32[]{:S(2)}, u32[]{:S(2)}) %collective-permute-start.5) | collective-permute-done | bytes 589856 | tf_op jit(solution)/shard_map/ppermute | solution.py:24
  115.9 8.8 %collective-permute-done.4 = bf16[4,2,48,768]{3,2,1,0:T(8,128)(2,1)S(1)} collective-permute-done((bf16[4,2,48,768]{3,2,1,0:T(8,128)(2,1)S(1)}, bf16[4,2,48,768]{3,2,1,0:T(8,128)(2,1)S(1)}, u32[]{:S(2)}, u32[]{:S(2)}) %collective-permute-start.4) | collective-permute-done | bytes 589856 | tf_op jit(solution)/shard_map/ppermute | solution.py:24
  131.2 5.2 convolution_bitcast_fusion
  142.5 30.2 %while.28 = (s32[]{:T(128)}, bf16[4,512,6,64]{1,3,2,0:T(8,128)(2,1)}, f32[4,6,512]{2,1,0:T(8,128)}, bf16[4,512,6,64]{1,3,2,0:T(8,128)(2,1)}, s32[4,512]{1,0:T(4,...) while((s32[]{:T(128)}, bf16[4,512,6,64]{1,3,2,0:T(8,128)(2,1)}, ...), condition=%wide.region_3.4_spmd.clone, body=%wide.region_0.3_spmd.sunk.clone | while | flops 421786624 | bytes 34590868 | solution.py:233
  172.7 5.5 fusion.149
  184.0 20.0 %add_convert_fusion.1 = bf16[4,512,6,64]{1,3,2,0:T(8,128)(2,1)} fusion(f32[4,512,6,64]{1,3,2,0:T(8,128)} %bitcast.626, f32[4,512,6]{1,2,0:T(8,128)S(1)} %copy.180, f32[4,512,6]{1,2,0:T(8,128)S(1)} %copy.179, f32[4,512,6]{1,2,0:T(8,128)S(1)} %copy.178, f32[4,512,6]{1,2,0:T(8,128)S(1)} %copy.177, f32[4,512,6]{1,2,0:T(8,128)S(1)} %copy.176, ...), kind=kLoop, calls=%fused_computation.242 | loop fusion | flops 14155776 | bytes 5160960 | tf_op jit(solution)/shard_map/convert.28
  208.9 5.9 fusion.206
  217.6 3.8 select_bitcast_fusion.1
  222.6 62.4 %fusion.61 = (bf16[4,512,2,1536]{3,1,0,2:T(8,128)(2,1)}, f32[4,512,2,1536]{3,1,0,2:T(8,128)}, f32[2,1536,4,512]{1,3,2,0:T(8,128)}) fusion(f32[2,1536]{1,0:T(2,128)S(1)} %copy-done.107, bf16[4,64,2,8,384]{4,3,2,1,0:T(8,128)(2,1)S(1)} %bitcast.660, bf16[2,1536,768]{2,1,0:T(8,128)(2,1)S(1)} %bitcast.650), kind=kOutput, calls=%fused_computation.78 | convolution fusion | flops 5247074304 | bytes 68431872 | tf_op jit(solution)/shard_map/rsgi,gij->rsgj/dot_general | solution.py:245
  285.0 11.2 %convolution_bitcast_fusion.1 = f32[4,512,2,384]{1,3,0,2:T(8,128)} fusion(bf16[4,512,2,1536]{3,1,0,2:T(8,128)(2,1)} %get-tuple-element.240, bf16[2,1536,768]{2,1,0:T(8,128)(2,1)S(1)} %bitcast.651), kind=kOutput, calls=%fused_computation.252 | convolution fusion | flops 4831838208 | bytes 21233664 | tf_op jit(solution)/shard_map/rsgj,gji->rsgi/dot_general | solution.py:253
  296.2 10.4 %copy.189 = f32[4,512,2,384]{3,2,1,0:T(2,128)} copy(f32[4,512,2,384]{1,3,0,2:T(8,128)} %convolution_bitcast_fusion.1) | data formatting | bytes 12582912 | tf_op jit(solution)/shard_map/rsgj,gji->rsgi/transpose | solution.py:253
  306.6 9.1 %reshape.582 = f32[4,512,768]{2,1,0:T(8,128)} reshape(f32[4,512,2,384]{3,2,1,0:T(2,128)} %copy.189) | data formatting | bytes 12582912 | tf_op jit(solution)/shard_map/reshape | solution.py:255
  315.7 5.7 fusion.199
  329.8 12.0 %bitcast_convert_fusion = bf16[2,1536,384]{2,1,0:T(8,128)(2,1)} fusion(bf16[4,512,2,1536]{3,1,0,2:T(8,128)(2,1)} %get-tuple-element.240, bf16[4,64,2,8,384]{4,3,2,1,0:T(8,128)(2,1)S(1)} %bitcast.662), kind=kOutput, calls=%fused_computation.197 | convolution fusion | flops 4833017856 | bytes 18087936 | tf_op jit(solution)/shard_map/rsgj,rsgi->gji/dot_general | solution.py:268
  341.8 26.6 %fusion.207 = (f32[2,1536]{1,0:T(2,128)S(1)}, bf16[4,512,2,1536]{3,1,0,2:T(8,128)(2,1)}) fusion(f32[4,512,2,1536]{3,1,0,2:T(8,128)} %get-tuple-element.241, bf16[4,64,2,8,384]{4,3,2,1,0:T(8,128)(2,1)} %bitcast.663, bf16[2,1536,768]{2,1,0:T(8,128)(2,1)S(1)} %bitcast.654, f32[2,1536,4,512]{1,3,2,0:T(8,128)} %get-tuple-element.350, f32[2,1536]{1,0:T(2,128)S(1)} %copy-done.107), kind=kOutput, calls=%fused_computation.495 | convolution fusion | flops 4932498432 | bytes 68444160 | tf_op jit(solution)/shard_map/rsgi,gji->rsgj/dot_general | solution.py:271
  368.4 11.8 %bitcast_convert_fusion.1 = bf16[2,1536,384]{2,1,0:T(8,128)(2,1)} fusion(bf16[4,512,2,1536]{3,1,0,2:T(8,128)(2,1)} %get-tuple-element.354, bf16[4,64,2,8,384]{4,3,2,1,0:T(8,128)(2,1)} %bitcast.661), kind=kOutput, calls=%fused_computation.198 | convolution fusion | flops 4833017856 | bytes 18087936 | tf_op jit(solution)/shard_map/rsgi,rsgj->gij/dot_general | solution.py:276
  380.2 11.1 %fusion.128 = f32[4,512,2,384]{1,3,0,2:T(8,128)} fusion(bf16[4,512,2,1536]{3,1,0,2:T(8,128)(2,1)} %get-tuple-element.354, bf16[2,1536,768]{2,1,0:T(8,128)(2,1)S(1)} %bitcast.655), kind=kOutput, calls=%fused_computation.253 | convolution fusion | flops 4831838208 | bytes 21233664 | tf_op jit(solution)/shard_map/rsgj,gij->rsgi/dot_general | solution.py:280
  391.2 10.3 %copy.192 = f32[4,512,2,384]{3,2,1,0:T(2,128)} copy(f32[4,512,2,384]{1,3,0,2:T(8,128)} %fusion.128) | data formatting | bytes 12582912 | tf_op jit(solution)/shard_map/rsgj,gij->rsgi/transpose | solution.py:280
  401.5 9.6 %reshape.584 = f32[4,512,768]{2,1,0:T(8,128)} reshape(f32[4,512,2,384]{3,2,1,0:T(2,128)} %copy.192) | data formatting | bytes 12582912 | tf_op jit(solution)/shard_map/reshape | solution.py:282
  411.2 12.0 %fusion.99 = (f32[768]{0:T(1024)S(1)}, f32[768]{0:T(1024)S(1)}, f32[768]{0:T(1024)S(1)}, f32[768]{0:T(1024)S(1)}, f32[4,512]{1,0:T(4,128)S(1)}, /*index=5*/f32[4...) fusion(bf16[4,512,768]{2,1,0:T(8,128)(2,1)} %param.21, ...), kind=kLoop, calls=%fused_computation.147 | loop fusion | flops 39313664 | bytes 31547392 | tf_op jit(solution)/shard_map/reduce_sum | solution.py:115
  428.1 4.1 convolution_convert_fusion
  434.3 4.4 fusion.202
  441.3 63.9 %while.29 = (s32[]{:T(128)}, f32[4,512,6,64]{1,3,2,0:T(8,128)}, bf16[4,512,6,64]{1,3,2,0:T(8,128)(2,1)}, f32[4,512,6,64]{1,3,2,0:T(8,128)}, bf16[4,512,6,64]{1,3...) while((s32[]{:T(128)}, f32[4,512,6,64]{1,3,2,0:T(8,128)}, ...), condition=%wide.region_26.27_spmd.clone, body=%wide.region_24.26_spmd.sunk.clone | while | flops 1030878208 | bytes 59743376 | solution.py:328
  505.2 4.4 fusion.201
  510.2 3.5 fusion.132
  515.5 3.6 copy.195
  519.2 25.9 %multiply_reduce_fusion.15 = (f32[4,512,6]{1,2,0:T(8,128)S(1)}, f32[4,512,6]{1,2,0:T(8,128)S(1)}, f32[4,512,6]{1,2,0:T(8,128)S(1)}, f32[4,512,6]{1,2,0:T(8,128)S...) fusion(f32[4,512,6,64]{1,3,2,0:T(8,128)} %bitcast.628, ...), kind=kLoop, calls=%fused_computation.233 | loop fusion | flops 20336640 | bytes 32292864 | tf_op jit(solution)/shard_map/reduce_sum | solution.py:297
  545.1 11.9 %fusion.196 = (f32[6,64]{1,0:T(8,128)S(1)}, bf16[4,512,6,64]{1,3,2,0:T(8,128)(2,1)}) fusion(f32[4,512,6,64]{1,3,2,0:T(8,128)} %get-tuple-element.281, f32[4,512,6,64]{1,3,2,0:T(8,128)} %get-tuple-element.280, f32[4,512,6,64]{1,3,2,0:T(8,128)} %get-tuple-element.279, f32[4,512,6,64]{1,3,2,0:T(8,128)} %get-tuple-element.278, ...), kind=kLoop, calls=%fused_computation.487 | loop fusion | flops 8650368 | bytes 29935104 | tf_op jit(solution)/shard_map/reduce_sum | solution.py:342
  566.1 5.9 fusion.195
  572.5 19.1 %multiply_multiply_fusion = (f32[4,512,768]{2,1,0:T(8,128)}, f32[4,512,768]{2,1,0:T(8,128)}, f32[4,512,768]{2,1,0:T(8,128)}, f32[4,512,768]{2,1,0:T(8,128)}, f32...) fusion(f32[4,512]{1,0:T(4,128)S(1)} %copy-done.66, ...), kind=kOutput, calls=%fused_computation.95 | convolution fusion | flops 1235484672 | bytes 62021632 | tf_op jit(solution)/shard_map/rse,de->rsd/dot_general | solution.py:315
  591.6 30.6 %multiply_reduce_fusion.2 = (f32[768]{0:T(1024)S(1)}, f32[768]{0:T(1024)S(1)}, f32[768]{0:T(1024)S(1)}, f32[768]{0:T(1024)S(1)}, f32[768]{0:T(1024)S(1)}, /*inde...) fusion(f32[4,512,768]{2,1,0:T(8,128)S(1)} %get-tuple-element.351, ...), kind=kLoop, calls=%fused_computation.150 | loop fusion | flops 44033280 | bytes 15830016 | tf_op jit(solution)/shard_map/reduce_sum | solution.py:323
  623.7 9.6 %bitcast_convert_fusion.2 = bf16[1536,768]{0,1:T(8,128)(2,1)S(1)} fusion(bf16[4,512,768]{2,1,0:T(8,128)(2,1)} %param.19, bf16[4,512,384]{1,2,0:T(8,128)(2,1)} %bitcast.673, bf16[4,512,384]{1,2,0:T(8,128)(2,1)} %bitcast.675, bf16[4,512,384]{1,2,0:T(8,128)(2,1)} %bitcast.640, bf16[4,512,384]{1,2,0:T(8,128)(2,1)} %get-tuple-element.234), kind=kOutput, calls=%fused_computation.199 | convolution fusion | flops 4858183680 | bytes 11796480 | tf_op jit(solution)/shard_map/rsd,rse->de/dot_general | solution.py:348
  633.3 28.1 %fusion.86 = f32[4,512,768]{2,1,0:T(8,128)} fusion(f32[4,512,768]{2,1,0:T(8,128)} %copy-done.19, f32[4,512,768]{2,1,0:T(8,128)} %get-tuple-element.262, f32[4,512,768]{2,1,0:T(8,128)} %get-tuple-element.261, f32[4,512,768]{2,1,0:T(8,128)} %get-tuple-element.260, f32[4,512,768]{2,1,0:T(8,128)} %get-tuple-element.259, ...), kind=kOutput, calls=%fused_computation.134 | convolution fusion | flops 4875878400 | bytes 77868032 | tf_op jit(solution)/shard_map/rse,de->rsd/dot_general | solution.py:349
  661.4 4.8 fusion.148
  671.1 4.3 collective-permute-done.44
  676.7 4.5 collective-permute-start.48
  685.8 8.5 %collective-permute-done.47 = f32[296,128]{1,0:T(8,128)S(1)} collective-permute-done((f32[296,128]{1,0:T(8,128)S(1)}, f32[296,128]{1,0:T(8,128)S(1)}, u32[]{:S(2)}, u32[]{:S(2)}) %collective-permute-start.47) | collective-permute-done | bytes 151584 | tf_op jit(solution)/shard_map/ppermute | solution.py:24
  696.3 4.8 collective-permute-done.31
  727.9 7.4 collective-permute-done.24
  741.3 6.2 collective-permute-done.36
  749.1 10.0 %collective-permute-done.38 = bf16[4,2,48,768]{3,2,1,0:T(8,128)(2,1)S(1)} collective-permute-done((bf16[4,2,48,768]{3,2,1,0:T(8,128)(2,1)S(1)}, bf16[4,2,48,768]{3,2,1,0:T(8,128)(2,1)S(1)}, u32[]{:S(2)}, u32[]{:S(2)}) %collective-permute-start.38) | collective-permute-done | bytes 589856 | tf_op jit(solution)/shard_map/ppermute | solution.py:24
  770.4 4.6 collective-permute-done.40
  (577 shorter events, 262.5 us)
Async XLA Ops:
  2.2 65.1 %collective-permute-start.16 = (bf16[1,24,768]{2,1,0:T(8,128)(2,1)}, bf16[1,24,768]{2,1,0:T(8,128)(2,1)}, u32[]{:S(2)}, u32[]{:S(2)}) collective-permute-start(bf16[1,24,768]{2,1,0:T(8,128)(2,1)} %convert_bitcast_fusion.3), channel_id=1, source_target_pairs={{0,8},{2,10},{4,12},{6,14},{8,0},{10,2},{12,4},{14,6},{16,24},{18,... | collective-permute-start | bytes 110600 | tf_op jit(solution)/shard_map/ppermute | solution.py:24
  5.2 62.1 %collective-permute-start.15 = (bf16[1,24,768]{2,1,0:T(8,128)(2,1)}, bf16[1,24,768]{2,1,0:T(8,128)(2,1)}, u32[]{:S(2)}, u32[]{:S(2)}) collective-permute-start(bf16[1,24,768]{2,1,0:T(8,128)(2,1)} %convert_bitcast_fusion.3), channel_id=1, source_target_pairs={{0,16},{2,18},{4,20},{6,22},{8,24},{10,26},{12,28},{14,30},{16,0},... | collective-permute-start | bytes 110600 | tf_op jit(solution)/shard_map/ppermute | solution.py:24
  7.8 60.1 %collective-permute-start.14 = (bf16[1,24,768]{2,1,0:T(8,128)(2,1)}, bf16[1,24,768]{2,1,0:T(8,128)(2,1)}, u32[]{:S(2)}, u32[]{:S(2)}) collective-permute-start(bf16[1,24,768]{2,1,0:T(8,128)(2,1)} %convert_bitcast_fusion.3), channel_id=1, source_target_pairs={{0,24},{2,26},{4,28},{6,30},{8,16},{10,18},{12,20},{14,22},{16,8},... | collective-permute-start | bytes 110600 | tf_op jit(solution)/shard_map/ppermute | solution.py:24
  10.2 62.6 %collective-permute-start.9 = (bf16[1,24,1920]{2,1,0:T(8,128)(2,1)}, bf16[1,24,1920]{2,1,0:T(8,128)(2,1)}, u32[]{:S(2)}, u32[]{:S(2)}) collective-permute-start(bf16[1,24,1920]{2,1,0:T(8,128)(2,1)} %pad_maximum_fusion.12), channel_id=1, source_target_pairs={{0,8},{2,10},{4,12},{6,14},{8,0},{10,2},{12,4},{14,6},{16,24},{18,... | collective-permute-start | bytes 276488 | tf_op jit(solution)/shard_map/ppermute | solution.py:24
  11.1 61.8 %collective-permute-start.8 = (bf16[1,24,1920]{2,1,0:T(8,128)(2,1)}, bf16[1,24,1920]{2,1,0:T(8,128)(2,1)}, u32[]{:S(2)}, u32[]{:S(2)}) collective-permute-start(bf16[1,24,1920]{2,1,0:T(8,128)(2,1)} %pad_maximum_fusion.12), channel_id=1, source_target_pairs={{0,16},{2,18},{4,20},{6,22},{8,24},{10,26},{12,28},{14,30},{16,0},... | collective-permute-start | bytes 276488 | tf_op jit(solution)/shard_map/ppermute | solution.py:24
  67.4 7.7 collective-permute-start.7
  67.4 11.3 %collective-permute-start.2 = (bf16[1,2,48,768]{3,2,1,0:T(8,128)(2,1)}, bf16[1,2,48,768]{3,2,1,0:T(8,128)(2,1)S(1)}, u32[]{:S(2)}, u32[]{:S(2)}) collective-permute-start(bf16[1,2,48,768]{3,2,1,0:T(8,128)(2,1)} %pad_maximum_fusion.11), channel_id=1, source_target_pairs={{0,8},{2,10},{4,12},{6,14},{8,0},{10,2},{12,4},{14,6},{16,24},{18,... | collective-permute-start | bytes 442376 | tf_op jit(solution)/shard_map/ppermute | solution.py:24
  67.9 15.9 %collective-permute-start.1 = (bf16[1,2,48,768]{3,2,1,0:T(8,128)(2,1)}, bf16[1,2,48,768]{3,2,1,0:T(8,128)(2,1)S(1)}, u32[]{:S(2)}, u32[]{:S(2)}) collective-permute-start(bf16[1,2,48,768]{3,2,1,0:T(8,128)(2,1)} %pad_maximum_fusion.11), channel_id=1, source_target_pairs={{0,16},{2,18},{4,20},{6,22},{8,24},{10,26},{12,28},{14,30},{16,0},... | collective-permute-start | bytes 442376 | tf_op jit(solution)/shard_map/ppermute | solution.py:24
  72.8 12.5 %collective-permute-start = (bf16[1,2,48,768]{3,2,1,0:T(8,128)(2,1)}, bf16[1,2,48,768]{3,2,1,0:T(8,128)(2,1)S(1)}, u32[]{:S(2)}, u32[]{:S(2)}) collective-permute-start(bf16[1,2,48,768]{3,2,1,0:T(8,128)(2,1)} %pad_maximum_fusion.11), channel_id=1, source_target_pairs={{0,24},{2,26},{4,28},{6,30},{8,16},{10,18},{12,20},{14,22},{16,8},... | collective-permute-start | bytes 442376 | tf_op jit(solution)/shard_map/ppermute | solution.py:24
  72.9 14.2 %collective-permute-start.19 = (bf16[4,24,768]{2,1,0:T(8,128)(2,1)S(1)}, bf16[4,24,768]{2,1,0:T(8,128)(2,1)S(1)}, u32[]{:S(2)}, u32[]{:S(2)}) collective-permute-start(bf16[4,24,768]{2,1,0:T(8,128)(2,1)S(1)} %maximum_bitcast_fusion.5), channel_id=1, source_target_pairs={{0,2},{2,0},{4,6},{6,4},{8,10},{10,8},{12,14},{14,12},{16,18},{18,... | collective-permute-start | bytes 442376 | tf_op jit(solution)/shard_map/ppermute | solution.py:24
  75.1 12.6 %collective-permute-start.18 = (bf16[4,24,768]{2,1,0:T(8,128)(2,1)S(1)}, bf16[4,24,768]{2,1,0:T(8,128)(2,1)S(1)}, u32[]{:S(2)}, u32[]{:S(2)}) collective-permute-start(bf16[4,24,768]{2,1,0:T(8,128)(2,1)S(1)} %maximum_bitcast_fusion.5), channel_id=1, source_target_pairs={{0,4},{2,6},{4,0},{6,2},{8,12},{10,14},{12,8},{14,10},{16,20},{18,... | collective-permute-start | bytes 442376 | tf_op jit(solution)/shard_map/ppermute | solution.py:24
  78.7 10.6 %collective-permute-start.17 = (bf16[4,24,768]{2,1,0:T(8,128)(2,1)S(1)}, bf16[4,24,768]{2,1,0:T(8,128)(2,1)S(1)}, u32[]{:S(2)}, u32[]{:S(2)}) collective-permute-start(bf16[4,24,768]{2,1,0:T(8,128)(2,1)S(1)} %maximum_bitcast_fusion.5), channel_id=1, source_target_pairs={{0,6},{2,4},{4,2},{6,0},{8,14},{10,12},{12,10},{14,8},{16,22},{18,... | collective-permute-start | bytes 442376 | tf_op jit(solution)/shard_map/ppermute | solution.py:24
  83.8 11.5 %collective-permute-start.12 = (bf16[4,24,1920]{2,1,0:T(8,128)(2,1)S(1)}, bf16[4,24,1920]{2,1,0:T(8,128)(2,1)S(1)}, u32[]{:S(2)}, u32[]{:S(2)}) collective-permute-start(bf16[4,24,1920]{2,1,0:T(8,128)(2,1)S(1)} %maximum_bitcast_fusion.4), channel_id=1, source_target_pairs={{0,2},{2,0},{4,6},{6,4},{8,10},{10,8},{12,14},{14,12},{16,18},{18,... | collective-permute-start | bytes 1105928 | tf_op jit(solution)/shard_map/ppermute | solution.py:24
  85.3 17.4 %collective-permute-start.11 = (bf16[4,24,1920]{2,1,0:T(8,128)(2,1)S(1)}, bf16[4,24,1920]{2,1,0:T(8,128)(2,1)S(1)}, u32[]{:S(2)}, u32[]{:S(2)}) collective-permute-start(bf16[4,24,1920]{2,1,0:T(8,128)(2,1)S(1)} %maximum_bitcast_fusion.4), channel_id=1, source_target_pairs={{0,4},{2,6},{4,0},{6,2},{8,12},{10,14},{12,8},{14,10},{16,20},{18,... | collective-permute-start | bytes 1105928 | tf_op jit(solution)/shard_map/ppermute | solution.py:24
  87.1 17.1 %collective-permute-start.10 = (bf16[4,24,1920]{2,1,0:T(8,128)(2,1)S(1)}, bf16[4,24,1920]{2,1,0:T(8,128)(2,1)S(1)}, u32[]{:S(2)}, u32[]{:S(2)}) collective-permute-start(bf16[4,24,1920]{2,1,0:T(8,128)(2,1)S(1)} %maximum_bitcast_fusion.4), channel_id=1, source_target_pairs={{0,6},{2,4},{4,2},{6,0},{8,14},{10,12},{12,10},{14,8},{16,22},{18,... | collective-permute-start | bytes 1105928 | tf_op jit(solution)/shard_map/ppermute | solution.py:24
  87.7 28.2 %collective-permute-start.5 = (bf16[4,2,48,768]{3,2,1,0:T(8,128)(2,1)S(1)}, bf16[4,2,48,768]{3,2,1,0:T(8,128)(2,1)S(1)}, u32[]{:S(2)}, u32[]{:S(2)}) collective-permute-start(bf16[4,2,48,768]{3,2,1,0:T(8,128)(2,1)S(1)} %maximum_bitcast_fusion.3), channel_id=1, source_target_pairs={{0,2},{2,0},{4,6},{6,4},{8,10},{10,8},{12,14},{14,12},{16,18},{18,... | collective-permute-start | bytes 1769480 | tf_op jit(solution)/shard_map/ppermute | solution.py:24
  89.3 35.4 %collective-permute-start.4 = (bf16[4,2,48,768]{3,2,1,0:T(8,128)(2,1)S(1)}, bf16[4,2,48,768]{3,2,1,0:T(8,128)(2,1)S(1)}, u32[]{:S(2)}, u32[]{:S(2)}) collective-permute-start(bf16[4,2,48,768]{3,2,1,0:T(8,128)(2,1)S(1)} %maximum_bitcast_fusion.3), channel_id=1, source_target_pairs={{0,4},{2,6},{4,0},{6,2},{8,12},{10,14},{12,8},{14,10},{16,20},{18,... | collective-permute-start | bytes 1769480 | tf_op jit(solution)/shard_map/ppermute | solution.py:24
  95.3 29.3 %collective-permute-start.3 = (bf16[4,2,48,768]{3,2,1,0:T(8,128)(2,1)S(1)}, bf16[4,2,48,768]{3,2,1,0:T(8,128)(2,1)S(1)}, u32[]{:S(2)}, u32[]{:S(2)}) collective-permute-start(bf16[4,2,48,768]{3,2,1,0:T(8,128)(2,1)S(1)} %maximum_bitcast_fusion.3), channel_id=1, source_target_pairs={{0,6},{2,4},{4,2},{6,0},{8,14},{10,12},{12,10},{14,8},{16,22},{18,... | collective-permute-start | bytes 1769480 | tf_op jit(solution)/shard_map/ppermute | solution.py:24
  104.8 23.3 %collective-permute-start.13 = (bf16[1,16,24,1920]{3,2,1,0:T(8,128)(2,1)S(1)}, bf16[1,16,24,1920]{3,2,1,0:T(8,128)(2,1)S(1)}, u32[]{:S(2)}, u32[]{:S(2)}) collective-permute-start(bf16[1,16,24,1920]{3,2,1,0:T(8,128)(2,1)S(1)} %bitcast.644), channel_id=1, source_target_pairs={{0,1},{1,0},{2,3},{3,2},{4,5},{5,4},{6,7},{7,6},{8,9},{9,8},{10,11... | collective-permute-start | bytes 4423688 | tf_op jit(solution)/shard_map/ppermute | solution.py:24
  105.0 21.8 %collective-permute-start.20 = (bf16[1,16,24,768]{3,2,1,0:T(8,128)(2,1)S(1)}, bf16[1,16,24,768]{3,2,1,0:T(8,128)(2,1)S(1)}, u32[]{:S(2)}, u32[]{:S(2)}) collective-permute-start(bf16[1,16,24,768]{3,2,1,0:T(8,128)(2,1)S(1)} %bitcast.666), channel_id=1, source_target_pairs={{0,1},{1,0},{2,3},{3,2},{4,5},{5,4},{6,7},{7,6},{8,9},{9,8},{10,11... | collective-permute-start | bytes 1769480 | tf_op jit(solution)/shard_map/ppermute | solution.py:24
  126.7 90.8 %collective-permute-start.6 = (bf16[1,16,2,48,768]{4,3,2,1,0:T(8,128)(2,1)}, bf16[1,16,2,48,768]{4,3,2,1,0:T(8,128)(2,1)}, u32[]{:S(2)}, u32[]{:S(2)}) collective-permute-start(bf16[1,16,2,48,768]{4,3,2,1,0:T(8,128)(2,1)} %bitcast.34), channel_id=1, source_target_pairs={{0,1},{1,0},{2,3},{3,2},{4,5},{5,4},{6,7},{7,6},{8,9},{9,8},{10,11... | collective-permute-start | bytes 7077896 | tf_op jit(solution)/shard_map/ppermute | solution.py:24
  433.8 249.1 %collective-permute-start.28 = (bf16[1,16,24,768]{3,2,1,0:T(8,128)(2,1)}, bf16[1,16,24,768]{3,2,1,0:T(8,128)(2,1)}, u32[]{:S(2)}, u32[]{:S(2)}) collective-permute-start(bf16[1,16,24,768]{3,2,1,0:T(8,128)(2,1)} %dynamic-slice_bitcast_fusion.4), channel_id=1, source_target_pairs={{0,1},{1,0},{2,3},{3,2},{4,5},{5,4},{6,7},{7,6},{8,9},{9,8},{10,11... | collective-permute-start | bytes 1769480 | tf_op jit(solution)/shard_map/ppermute | solution.py:24
  515.5 203.4 %collective-permute-start.35 = (bf16[1,16,2,48,768]{4,3,2,1,0:T(8,128)(2,1)}, bf16[1,16,2,48,768]{4,3,2,1,0:T(8,128)(2,1)}, u32[]{:S(2)}, u32[]{:S(2)}) collective-permute-start(bf16[1,16,2,48,768]{4,3,2,1,0:T(8,128)(2,1)} %bitcast.553), channel_id=1, source_target_pairs={{0,1},{1,0},{2,3},{3,2},{4,5},{5,4},{6,7},{7,6},{8,9},{9,8},{10,11... | collective-permute-start | bytes 7077896 | tf_op jit(solution)/shard_map/ppermute | solution.py:24
  623.2 43.0 %collective-permute-start.42 = (f32[296,128]{1,0:T(8,128)}, f32[296,128]{1,0:T(8,128)S(1)}, u32[]{:S(2)}, u32[]{:S(2)}) collective-permute-start(f32[296,128]{1,0:T(8,128)} %pad_bitcast_fusion), channel_id=1, source_target_pairs={{0,1},{1,0},{2,3},{3,2},{4,5},{5,4},{6,7},{7,6},{8,9},{9,8},{10,11... | collective-permute-start | bytes 454664 | tf_op jit(solution)/shard_map/ppermute | solution.py:24
  666.3 9.0 %collective-permute-start.44 = (f32[296,128]{1,0:T(8,128)S(1)}, f32[296,128]{1,0:T(8,128)S(1)}, u32[]{:S(2)}, u32[]{:S(2)}) collective-permute-start(f32[296,128]{1,0:T(8,128)S(1)} %fusion.187), channel_id=1, source_target_pairs={{0,4},{2,6},{4,0},{6,2},{8,12},{10,14},{12,8},{14,10},{16,20},{18,... | collective-permute-start | bytes 454664 | tf_op jit(solution)/shard_map/ppermute | solution.py:24
  667.9 7.7 collective-permute-start.45
  669.1 7.6 collective-permute-start.43
  675.3 37.7 %collective-permute-start.21 = (bf16[1,16,24,1920]{3,2,1,0:T(8,128)(2,1)}, bf16[1,16,24,1920]{3,2,1,0:T(8,128)(2,1)}, u32[]{:S(2)}, u32[]{:S(2)}) collective-permute-start(bf16[1,16,24,1920]{3,2,1,0:T(8,128)(2,1)} %fusion.145), channel_id=1, source_target_pairs={{0,1},{1,0},{2,3},{3,2},{4,5},{5,4},{6,7},{7,6},{8,9},{9,8},{10,11... | collective-permute-start | bytes 4423688 | tf_op jit(solution)/shard_map/ppermute | solution.py:24
  676.7 8.9 %collective-permute-start.48 = (f32[296,128]{1,0:T(8,128)S(1)}, f32[296,128]{1,0:T(8,128)S(1)}, u32[]{:S(2)}, u32[]{:S(2)}) collective-permute-start(f32[296,128]{1,0:T(8,128)S(1)} %add_add_fusion.3), channel_id=1, source_target_pairs={{0,24},{2,26},{4,28},{6,30},{8,16},{10,18},{12,20},{14,22},{16,8},... | collective-permute-start | bytes 454664 | tf_op jit(solution)/shard_map/ppermute | solution.py:24
  681.2 13.1 %collective-permute-start.47 = (f32[296,128]{1,0:T(8,128)S(1)}, f32[296,128]{1,0:T(8,128)S(1)}, u32[]{:S(2)}, u32[]{:S(2)}) collective-permute-start(f32[296,128]{1,0:T(8,128)S(1)} %add_add_fusion.3), channel_id=1, source_target_pairs={{0,16},{2,18},{4,20},{6,22},{8,24},{10,26},{12,28},{14,30},{16,0},... | collective-permute-start | bytes 454664 | tf_op jit(solution)/shard_map/ppermute | solution.py:24
  683.0 12.7 %collective-permute-start.46 = (f32[296,128]{1,0:T(8,128)S(1)}, f32[296,128]{1,0:T(8,128)S(1)}, u32[]{:S(2)}, u32[]{:S(2)}) collective-permute-start(f32[296,128]{1,0:T(8,128)S(1)} %add_add_fusion.3), channel_id=1, source_target_pairs={{0,8},{2,10},{4,12},{6,14},{8,0},{10,2},{12,4},{14,6},{16,24},{18,... | collective-permute-start | bytes 454664 | tf_op jit(solution)/shard_map/ppermute | solution.py:24
  685.6 10.7 %collective-permute-start.29 = (bf16[4,24,768]{2,1,0:T(8,128)(2,1)S(1)}, bf16[4,24,768]{2,1,0:T(8,128)(2,1)S(1)}, u32[]{:S(2)}, u32[]{:S(2)}) collective-permute-start(bf16[4,24,768]{2,1,0:T(8,128)(2,1)S(1)} %get-tuple-element.303), channel_id=1, source_target_pairs={{0,2},{2,0},{4,6},{6,4},{8,10},{10,8},{12,14},{14,12},{16,18},{18,... | collective-permute-start | bytes 442376 | tf_op jit(solution)/shard_map/ppermute | solution.py:24
  694.3 6.8 collective-permute-start.31
  695.7 8.3 %collective-permute-start.30 = (bf16[4,24,768]{2,1,0:T(8,128)(2,1)S(1)}, bf16[4,24,768]{2,1,0:T(8,128)(2,1)S(1)}, u32[]{:S(2)}, u32[]{:S(2)}) collective-permute-start(bf16[4,24,768]{2,1,0:T(8,128)(2,1)S(1)} %get-tuple-element.305), channel_id=1, source_target_pairs={{0,4},{2,6},{4,0},{6,2},{8,12},{10,14},{12,8},{14,10},{16,20},{18,... | collective-permute-start | bytes 442376 | tf_op jit(solution)/shard_map/ppermute | solution.py:24
  704.1 8.3 %collective-permute-start.32 = (bf16[1,24,768]{2,1,0:T(8,128)(2,1)S(1)}, bf16[1,24,768]{2,1,0:T(8,128)(2,1)S(1)}, u32[]{:S(2)}, u32[]{:S(2)}) collective-permute-start(bf16[1,24,768]{2,1,0:T(8,128)(2,1)S(1)} %get-tuple-element.332), channel_id=1, source_target_pairs={{0,8},{2,10},{4,12},{6,14},{8,0},{10,2},{12,4},{14,6},{16,24},{18,... | collective-permute-start | bytes 110600 | tf_op jit(solution)/shard_map/ppermute | solution.py:24
  704.2 8.2 %collective-permute-start.34 = (bf16[1,24,768]{2,1,0:T(8,128)(2,1)S(1)}, bf16[1,24,768]{2,1,0:T(8,128)(2,1)S(1)}, u32[]{:S(2)}, u32[]{:S(2)}) collective-permute-start(bf16[1,24,768]{2,1,0:T(8,128)(2,1)S(1)} %get-tuple-element.333), channel_id=1, source_target_pairs={{0,24},{2,26},{4,28},{6,30},{8,16},{10,18},{12,20},{14,22},{16,8},... | collective-permute-start | bytes 110600 | tf_op jit(solution)/shard_map/ppermute | solution.py:24
  715.3 11.6 %collective-permute-start.22 = (bf16[4,24,1920]{2,1,0:T(8,128)(2,1)S(1)}, bf16[4,24,1920]{2,1,0:T(8,128)(2,1)S(1)}, u32[]{:S(2)}, u32[]{:S(2)}) collective-permute-start(bf16[4,24,1920]{2,1,0:T(8,128)(2,1)S(1)} %get-tuple-element.291), channel_id=1, source_target_pairs={{0,2},{2,0},{4,6},{6,4},{8,10},{10,8},{12,14},{14,12},{16,18},{18,... | collective-permute-start | bytes 1105928 | tf_op jit(solution)/shard_map/ppermute | solution.py:24
  716.6 18.7 %collective-permute-start.24 = (bf16[4,24,1920]{2,1,0:T(8,128)(2,1)S(1)}, bf16[4,24,1920]{2,1,0:T(8,128)(2,1)S(1)}, u32[]{:S(2)}, u32[]{:S(2)}) collective-permute-start(bf16[4,24,1920]{2,1,0:T(8,128)(2,1)S(1)} %get-tuple-element.292), channel_id=1, source_target_pairs={{0,6},{2,4},{4,2},{6,0},{8,14},{10,12},{12,10},{14,8},{16,22},{18,... | collective-permute-start | bytes 1105928 | tf_op jit(solution)/shard_map/ppermute | solution.py:24
  717.8 19.4 %collective-permute-start.23 = (bf16[4,24,1920]{2,1,0:T(8,128)(2,1)S(1)}, bf16[4,24,1920]{2,1,0:T(8,128)(2,1)S(1)}, u32[]{:S(2)}, u32[]{:S(2)}) collective-permute-start(bf16[4,24,1920]{2,1,0:T(8,128)(2,1)S(1)} %get-tuple-element.293), channel_id=1, source_target_pairs={{0,4},{2,6},{4,0},{6,2},{8,12},{10,14},{12,8},{14,10},{16,20},{18,... | collective-permute-start | bytes 1105928 | tf_op jit(solution)/shard_map/ppermute | solution.py:24
  721.4 26.1 %collective-permute-start.36 = (bf16[4,2,48,768]{3,2,1,0:T(8,128)(2,1)S(1)}, bf16[4,2,48,768]{3,2,1,0:T(8,128)(2,1)S(1)}, u32[]{:S(2)}, u32[]{:S(2)}) collective-permute-start(bf16[4,2,48,768]{3,2,1,0:T(8,128)(2,1)S(1)} %get-tuple-element.284), channel_id=1, source_target_pairs={{0,2},{2,0},{4,6},{6,4},{8,10},{10,8},{12,14},{14,12},{16,18},{18,... | collective-permute-start | bytes 1769480 | tf_op jit(solution)/shard_map/ppermute | solution.py:24
  722.7 36.4 %collective-permute-start.38 = (bf16[4,2,48,768]{3,2,1,0:T(8,128)(2,1)S(1)}, bf16[4,2,48,768]{3,2,1,0:T(8,128)(2,1)S(1)}, u32[]{:S(2)}, u32[]{:S(2)}) collective-permute-start(bf16[4,2,48,768]{3,2,1,0:T(8,128)(2,1)S(1)} %get-tuple-element.285), channel_id=1, source_target_pairs={{0,6},{2,4},{4,2},{6,0},{8,14},{10,12},{12,10},{14,8},{16,22},{18,... | collective-permute-start | bytes 1769480 | tf_op jit(solution)/shard_map/ppermute | solution.py:24
  726.9 33.5 %collective-permute-start.37 = (bf16[4,2,48,768]{3,2,1,0:T(8,128)(2,1)S(1)}, bf16[4,2,48,768]{3,2,1,0:T(8,128)(2,1)S(1)}, u32[]{:S(2)}, u32[]{:S(2)}) collective-permute-start(bf16[4,2,48,768]{3,2,1,0:T(8,128)(2,1)S(1)} %get-tuple-element.286), channel_id=1, source_target_pairs={{0,4},{2,6},{4,0},{6,2},{8,12},{10,14},{12,8},{14,10},{16,20},{18,... | collective-permute-start | bytes 1769480 | tf_op jit(solution)/shard_map/ppermute | solution.py:24
  737.5 27.2 %collective-permute-start.25 = (bf16[1,24,1920]{2,1,0:T(8,128)(2,1)S(1)}, bf16[1,24,1920]{2,1,0:T(8,128)(2,1)S(1)}, u32[]{:S(2)}, u32[]{:S(2)}) collective-permute-start(bf16[1,24,1920]{2,1,0:T(8,128)(2,1)S(1)} %get-tuple-element.322), channel_id=1, source_target_pairs={{0,8},{2,10},{4,12},{6,14},{8,0},{10,2},{12,4},{14,6},{16,24},{18,... | collective-permute-start | bytes 276488 | tf_op jit(solution)/shard_map/ppermute | solution.py:24
  738.3 26.4 %collective-permute-start.27 = (bf16[1,24,1920]{2,1,0:T(8,128)(2,1)S(1)}, bf16[1,24,1920]{2,1,0:T(8,128)(2,1)S(1)}, u32[]{:S(2)}, u32[]{:S(2)}) collective-permute-start(bf16[1,24,1920]{2,1,0:T(8,128)(2,1)S(1)} %get-tuple-element.323), channel_id=1, source_target_pairs={{0,24},{2,26},{4,28},{6,30},{8,16},{10,18},{12,20},{14,22},{16,8},... | collective-permute-start | bytes 276488 | tf_op jit(solution)/shard_map/ppermute | solution.py:24
  747.5 17.3 %collective-permute-start.26 = (bf16[1,24,1920]{2,1,0:T(8,128)(2,1)S(1)}, bf16[1,24,1920]{2,1,0:T(8,128)(2,1)S(1)}, u32[]{:S(2)}, u32[]{:S(2)}) collective-permute-start(bf16[1,24,1920]{2,1,0:T(8,128)(2,1)S(1)} %get-tuple-element.324), channel_id=1, source_target_pairs={{0,16},{2,18},{4,20},{6,22},{8,24},{10,26},{12,28},{14,30},{16,0},... | collective-permute-start | bytes 276488 | tf_op jit(solution)/shard_map/ppermute | solution.py:24
  760.7 6.8 collective-permute-start.39
  761.6 8.8 %collective-permute-start.41 = (bf16[1,2,48,768]{3,2,1,0:T(8,128)(2,1)S(1)}, bf16[1,2,48,768]{3,2,1,0:T(8,128)(2,1)S(1)}, u32[]{:S(2)}, u32[]{:S(2)}) collective-permute-start(bf16[1,2,48,768]{3,2,1,0:T(8,128)(2,1)S(1)} %get-tuple-element.301), channel_id=1, source_target_pairs={{0,24},{2,26},{4,28},{6,30},{8,16},{10,18},{12,20},{14,22},{16,8},... | collective-permute-start | bytes 442376 | tf_op jit(solution)/shard_map/ppermute | solution.py:24
  764.7 10.4 %collective-permute-start.40 = (bf16[1,2,48,768]{3,2,1,0:T(8,128)(2,1)S(1)}, bf16[1,2,48,768]{3,2,1,0:T(8,128)(2,1)S(1)}, u32[]{:S(2)}, u32[]{:S(2)}) collective-permute-start(bf16[1,2,48,768]{3,2,1,0:T(8,128)(2,1)S(1)} %get-tuple-element.302), channel_id=1, source_target_pairs={{0,16},{2,18},{4,20},{6,22},{8,24},{10,26},{12,28},{14,30},{16,0},... | collective-permute-start | bytes 442376 | tf_op jit(solution)/shard_map/ppermute | solution.py:24
  (132 other events, 2642.3 us)
